TPU v7x, 32 devices: a whole 2x2x4 slice. The times are simulated.
32 devices in a mesh: dp: 8 (over y, x, core), mp: 4 (over z).
Axes of the slice: x: 2, y: 2, z: 4, core: 2. Of those that a mesh axis runs over, the one named last changes fastest.
Arguments:
- tokens: bfloat16 [3, 8192, 1024], P(None, ('dp', 'mp')), may hold values from -6 to 6
- segment_ids: int32 [3, 8192], P(None, 'dp'), may hold values from 0 to 63, never falling along the last dimension, each value on 1 to 1024 neighbouring positions
- row_lengths: int32 [3, 8], P(None, 'dp'), may hold values from 512 to 1024, as said below
- ln1_gain: float32 [1024], replicated, may hold values from 0.5 to 1.5
- ln1_bias: float32 [1024], replicated, may hold values from -4 to 4
- qkv_weight: bfloat16 [1024, 3072], P(None, 'mp'), may hold values from -0.1875 to 0.1875
- qkv_bias: float32 [3072], P('mp'), may hold values from -4 to 4
- out_weight: bfloat16 [1024, 1024], P('mp'), may hold values from -0.75 to 0.75
- out_bias: float32 [1024], replicated, may hold values from -4 to 4
- ln2_gain: float32 [1024], replicated, may hold values from 0.5 to 1.5
- ln2_bias: float32 [1024], replicated, may hold values from -4 to 4
- up_weight: bfloat16 [1024, 4096], P(None, 'mp'), may hold values from -0.1875 to 0.1875
- up_bias: float32 [4096], P('mp'), may hold values from -4 to 4
- down_weight: bfloat16 [4096, 1024], P('mp'), may hold values from -0.09375 to 0.09375
- down_bias: float32 [1024], replicated, may hold values from -4 to 4
- prefix_embed: bfloat16 [10, 1024], replicated, may hold values from -6 to 6
- reparam_in: bfloat16 [1024, 512], replicated, may hold values from -0.1875 to 0.1875
- reparam_in_bias: float32 [512], replicated, may hold values from -4 to 4
- reparam_out: bfloat16 [512, 2048], P(None, ('mp', 'dp')), may hold values from -0.25 to 0.25
- reparam_out_bias: float32 [2048], P(('mp', 'dp')), may hold values from -4 to 4
- cotangent: bfloat16 [3, 8192, 1024], P(None, ('dp', 'mp')), may hold values from -6 to 6
Outputs:
- block_out: bfloat16 [3, 8192, 1024], P(None, ('dp', 'mp'))
- input_grad: float32 [3, 8192, 1024], P(None, ('dp', 'mp'))
- ln1_gain_grad: float32 [1024], replicated
- ln1_bias_grad: float32 [1024], replicated
- qkv_weight_grad: float32 [1024, 3072], P(None, 'mp')
- qkv_bias_grad: float32 [3072], P('mp')
- out_weight_grad: float32 [1024, 1024], P('mp')
- out_bias_grad: float32 [1024], replicated
- ln2_gain_grad: float32 [1024], replicated
- ln2_bias_grad: float32 [1024], replicated
- up_weight_grad: float32 [1024, 4096], P(None, 'mp')
- up_bias_grad: float32 [4096], P('mp')
- down_weight_grad: float32 [4096, 1024], P('mp')
- down_bias_grad: float32 [1024], replicated
- prefix_embed_grad: float32 [10, 1024], replicated
- reparam_in_grad: float32 [1024, 512], replicated
- reparam_in_bias_grad: float32 [512], replicated
- reparam_out_grad: float32 [512, 2048], P(None, ('mp', 'dp'))
- reparam_out_bias_grad: float32 [2048], P(('mp', 'dp'))
Inputs may be any that keep to these rules, and one draw needn't show every extreme that they name: `segment_ids`: within each micro-batch the numbers never fall along the tokens; each number covers 1 to 1024 consecutive tokens, and every number of the range occurs. `row_lengths`: the first packed row of every micro-batch is full and the last one is half full.
All inputs are finite; a program needn't handle non-finite values.
Results may differ from a plain program's by a relative error of at most 0.02.
Values may be sent and summed in bfloat16 or wider, within the bound.
A program may use at most 192 MiB of HBM per device.

v0:
```python
import math

import jax
import jax.numpy as jnp
from jax import lax
from jax.sharding import PartitionSpec as P

HEAD_DIM = 64


EPSILON = 1e-05
MASKED = -1e30
HIGHEST = lax.Precision.HIGHEST


def normalize(inputs):
    average = jnp.mean(inputs, -1, keepdims=True)
    centered = inputs - average
    variance = jnp.mean(centered * centered, -1, keepdims=True)
    inverse = lax.rsqrt(variance + EPSILON)
    return (centered * inverse, inverse)


def norm_back(grad_norm, normed_hat, inverse, norm_gain):
    scaled = grad_norm * norm_gain
    return inverse * (
        scaled
        - jnp.mean(scaled, -1, keepdims=True)
        - normed_hat * jnp.mean(scaled * normed_hat, -1, keepdims=True)
    )


def product_transposed(rows_in, matrix):
    return lax.dot_general(
        rows_in, matrix, (((1,), (1,)), ((), ())), preferred_element_type=jnp.float32
    )


def outer_sum(left, right):
    return lax.dot_general(
        left, right, (((0,), (0,)), ((), ())), preferred_element_type=jnp.float32
    )


def gelu_tanh(values_in):
    return jax.nn.gelu(values_in, approximate=True)


def attention_scores(queries, keys_tok, keys_pre, visible, log_total):
    score_scale = 1.0 / math.sqrt(queries.shape[-1])
    scores_tok = (
        jnp.einsum("hqd,hkd->hqk", queries, keys_tok, preferred_element_type=jnp.float32)
        * score_scale
    )
    scores_tok = jnp.where(visible[None], scores_tok, MASKED)
    scores_pre = (
        jnp.einsum("hqd,hkd->hqk", queries, keys_pre, preferred_element_type=jnp.float32)
        * score_scale
    )
    if log_total is None:
        highest = jnp.maximum(
            jnp.max(scores_tok, -1, keepdims=True), jnp.max(scores_pre, -1, keepdims=True)
        )
        totals = jnp.sum(jnp.exp(scores_tok - highest), -1, keepdims=True) + jnp.sum(
            jnp.exp(scores_pre - highest), -1, keepdims=True
        )
        log_total = highest + jnp.log(totals)
    return (jnp.exp(scores_tok - log_total), jnp.exp(scores_pre - log_total), log_total)


def per_device(
    tokens,
    segment_ids,
    row_lengths,
    ln1_gain,
    ln1_bias,
    qkv_weight,
    qkv_bias,
    out_weight,
    out_bias,
    ln2_gain,
    ln2_bias,
    up_weight,
    up_bias,
    down_weight,
    down_bias,
    prefix_embed,
    reparam_in,
    reparam_in_bias,
    reparam_out,
    reparam_out_bias,
    cotangent,
):
    width_head = out_weight.shape[0]
    heads_local = width_head // HEAD_DIM
    prefix_slots = prefix_embed.shape[0]
    pre_act = (
        jnp.dot(prefix_embed, reparam_in, preferred_element_type=jnp.float32) + reparam_in_bias
    )
    tanh_hidden = jnp.tanh(pre_act)
    tanh_low = tanh_hidden.astype(jnp.bfloat16)
    table_part = (
        jnp.dot(tanh_low, reparam_out, preferred_element_type=jnp.float32) + reparam_out_bias
    ).astype(jnp.bfloat16)

    def micro_step(carried, inputs):
        big_sums, small_sums, table_grad = carried
        tokens_mb, segments_mb, length_mb, cotangent_mb = inputs
        table_full = lax.all_gather(table_part, "dp", axis=1, tiled=True)
        seq_len = segments_mb.shape[0]
        table_heads = table_full.reshape(prefix_slots, heads_local, 2, HEAD_DIM).transpose(
            2, 1, 0, 3
        )
        positions = jnp.arange(seq_len)
        visible = (
            (segments_mb[:, None] == segments_mb[None, :])
            & (positions[None, :] <= positions[:, None])
            & (positions[None, :] < length_mb)
        )
        x_share = tokens_mb.astype(jnp.float32)
        hat_first, inverse_first = normalize(x_share)
        normed_first = lax.all_gather(
            (hat_first * ln1_gain + ln1_bias).astype(jnp.bfloat16), "mp", axis=0, tiled=True
        )
        qkv_low = (
            jnp.dot(normed_first, qkv_weight, preferred_element_type=jnp.float32) + qkv_bias
        ).astype(jnp.bfloat16)
        packed = qkv_low.reshape(seq_len, heads_local, 3, HEAD_DIM).transpose(2, 1, 0, 3)
        weights_tok, weights_pre, log_total = attention_scores(
            packed[0], packed[1], table_heads[0], visible, None
        )
        heads_out = (
            jnp.einsum(
                "hqk,hkd->hqd",
                weights_tok.astype(jnp.bfloat16),
                packed[2],
                preferred_element_type=jnp.float32,
            )
            + jnp.einsum(
                "hqk,hkd->hqd",
                weights_pre.astype(jnp.bfloat16),
                table_heads[1],
                preferred_element_type=jnp.float32,
            )
        ).astype(jnp.bfloat16)
        head_rows = heads_out.transpose(1, 0, 2).reshape(seq_len, width_head)
        resid = (
            x_share
            + lax.psum_scatter(
                jnp.dot(head_rows, out_weight, preferred_element_type=jnp.float32).astype(
                    jnp.bfloat16
                ),
                "mp",
                scatter_dimension=0,
                tiled=True,
            ).astype(jnp.float32)
            + out_bias
        )
        hat_second, inverse_second = normalize(resid)
        normed_second = lax.all_gather(
            (hat_second * ln2_gain + ln2_bias).astype(jnp.bfloat16), "mp", axis=0, tiled=True
        )
        up_act = jnp.dot(normed_second, up_weight, preferred_element_type=jnp.float32) + up_bias
        gelu_out, gelu_back = jax.vjp(gelu_tanh, up_act)
        hidden_low = gelu_out.astype(jnp.bfloat16)
        block_share = (
            resid
            + lax.psum_scatter(
                jnp.dot(hidden_low, down_weight, preferred_element_type=jnp.float32).astype(
                    jnp.bfloat16
                ),
                "mp",
                scatter_dimension=0,
                tiled=True,
            ).astype(jnp.float32)
            + down_bias
        ).astype(jnp.bfloat16)
        cot_full = lax.all_gather(cotangent_mb, "mp", axis=0, tiled=True)
        d_up = gelu_back(product_transposed(cot_full, down_weight))[0].astype(jnp.bfloat16)
        grad_down = outer_sum(hidden_low, cot_full)
        grad_up = outer_sum(normed_second, d_up)
        grad_up_bias = jnp.sum(d_up.astype(jnp.float32), 0)
        d_second = lax.psum_scatter(
            product_transposed(d_up, up_weight).astype(jnp.bfloat16),
            "mp",
            scatter_dimension=0,
            tiled=True,
        ).astype(jnp.float32)
        cot_share = cotangent_mb.astype(jnp.float32)
        d_resid = cot_share + norm_back(d_second, hat_second, inverse_second, ln2_gain)
        d_attn = lax.all_gather(d_resid.astype(jnp.bfloat16), "mp", axis=0, tiled=True)
        grad_out = outer_sum(head_rows, d_attn)
        d_heads = (
            product_transposed(d_attn, out_weight)
            .astype(jnp.bfloat16)
            .reshape(seq_len, heads_local, HEAD_DIM)
            .transpose(1, 0, 2)
        )
        weights_tok, weights_pre, unused_total = attention_scores(
            packed[0], packed[1], table_heads[0], visible, log_total
        )
        score_scale = 1.0 / math.sqrt(HEAD_DIM)
        d_vtok = jnp.einsum(
            "hqk,hqd->hkd",
            weights_tok.astype(jnp.bfloat16),
            d_heads,
            preferred_element_type=jnp.float32,
        )
        d_vpre = jnp.einsum(
            "hqk,hqd->hkd",
            weights_pre.astype(jnp.bfloat16),
            d_heads,
            preferred_element_type=jnp.float32,
        )
        dprob_tok = jnp.einsum(
            "hqd,hkd->hqk", d_heads, packed[2], preferred_element_type=jnp.float32
        )
        dprob_pre = jnp.einsum(
            "hqd,hkd->hqk", d_heads, table_heads[1], preferred_element_type=jnp.float32
        )
        delta = jnp.sum(weights_tok * dprob_tok, -1, keepdims=True) + jnp.sum(
            weights_pre * dprob_pre, -1, keepdims=True
        )
        dscore_tok = (weights_tok * (dprob_tok - delta)).astype(jnp.bfloat16)
        dscore_pre = (weights_pre * (dprob_pre - delta)).astype(jnp.bfloat16)
        d_queries = (
            jnp.einsum("hqk,hkd->hqd", dscore_tok, packed[1], preferred_element_type=jnp.float32)
            + jnp.einsum(
                "hqk,hkd->hqd", dscore_pre, table_heads[0], preferred_element_type=jnp.float32
            )
        ) * score_scale
        d_ktok = (
            jnp.einsum("hqk,hqd->hkd", dscore_tok, packed[0], preferred_element_type=jnp.float32)
            * score_scale
        )
        d_kpre = (
            jnp.einsum("hqk,hqd->hkd", dscore_pre, packed[0], preferred_element_type=jnp.float32)
            * score_scale
        )
        prefix_add = (
            jnp.stack([d_kpre, d_vpre], 0)
            .transpose(2, 1, 0, 3)
            .reshape(prefix_slots, 2 * width_head)
        )
        d_qkv = (
            jnp.stack([d_queries, d_ktok, d_vtok], 0)
            .transpose(2, 1, 0, 3)
            .reshape(seq_len, 3 * width_head)
            .astype(jnp.bfloat16)
        )
        grad_qkv = outer_sum(normed_first, d_qkv)
        grad_qkv_bias = jnp.sum(d_qkv.astype(jnp.float32), 0)
        d_first = lax.psum_scatter(
            product_transposed(d_qkv, qkv_weight).astype(jnp.bfloat16),
            "mp",
            scatter_dimension=0,
            tiled=True,
        ).astype(jnp.float32)
        input_grad = d_resid + norm_back(d_first, hat_first, inverse_first, ln1_gain)
        small_add = (
            jnp.sum(d_first * hat_first, 0),
            jnp.sum(d_first, 0),
            jnp.sum(d_second * hat_second, 0),
            jnp.sum(d_second, 0),
            jnp.sum(d_resid, 0),
            jnp.sum(cot_share, 0),
        )
        big_add = (
            lax.psum(grad_qkv.astype(jnp.bfloat16), "dp").astype(jnp.float32),
            lax.psum(grad_qkv_bias.astype(jnp.bfloat16), "dp").astype(jnp.float32),
            lax.psum(grad_out.astype(jnp.bfloat16), "dp").astype(jnp.float32),
            lax.psum(grad_up.astype(jnp.bfloat16), "dp").astype(jnp.float32),
            lax.psum(grad_up_bias.astype(jnp.bfloat16), "dp").astype(jnp.float32),
            lax.psum(grad_down.astype(jnp.bfloat16), "dp").astype(jnp.float32),
        )
        big_sums = jax.tree.map(jnp.add, big_sums, tuple(big_add))
        small_sums = jax.tree.map(jnp.add, small_sums, small_add)
        return ((big_sums, small_sums, table_grad + prefix_add), (block_share, input_grad))

    big_zero = tuple(
        (
            jnp.zeros(member.shape, jnp.float32)
            for member in (qkv_weight, qkv_bias, out_weight, up_weight, up_bias, down_weight)
        )
    )
    small_zero = tuple((jnp.zeros(ln1_gain.shape, jnp.float32) for member in range(6)))
    table_zero = jnp.zeros((prefix_slots, 2 * width_head), jnp.float32)
    carried, stacked = lax.scan(
        micro_step,
        (big_zero, small_zero, table_zero),
        (tokens, segment_ids, row_lengths[:, 0], cotangent),
    )
    big_sums, small_sums, table_grad = carried
    block_out, input_grad = stacked
    table_own = lax.psum_scatter(table_grad, "dp", scatter_dimension=1, tiled=True)
    grad_rout = jnp.dot(tanh_low.astype(jnp.float32).T, table_own, precision=HIGHEST)
    grad_rout_bias = jnp.sum(table_own, 0)
    tanh_part = jnp.dot(table_own, reparam_out.astype(jnp.float32).T, precision=HIGHEST)
    shared = lax.psum(
        (
            tanh_part,
            small_sums[0],
            small_sums[1],
            small_sums[2],
            small_sums[3],
            small_sums[4],
            small_sums[5],
        ),
        ("dp", "mp"),
    )
    d_pre = shared[0] * (1.0 - tanh_hidden * tanh_hidden)
    grad_rin = jnp.dot(prefix_embed.astype(jnp.float32).T, d_pre, precision=HIGHEST)
    grad_rin_bias = jnp.sum(d_pre, 0)
    grad_embed = jnp.dot(d_pre, reparam_in.astype(jnp.float32).T, precision=HIGHEST)
    return (
        block_out,
        input_grad,
        shared[1],
        shared[2],
        big_sums[0],
        big_sums[1],
        big_sums[2],
        shared[5],
        shared[3],
        shared[4],
        big_sums[3],
        big_sums[4],
        big_sums[5],
        shared[6],
        grad_embed,
        grad_rin,
        grad_rin_bias,
        grad_rout,
        grad_rout_bias,
    )


def solution(mesh):
    placed = (
        P(None, ("dp", "mp"), None),
        P(None, "dp"),
        P(None, "dp"),
        P(),
        P(),
        P(None, "mp"),
        P("mp"),
        P("mp", None),
        P(),
        P(),
        P(),
        P(None, "mp"),
        P("mp"),
        P("mp", None),
        P(),
        P(),
        P(),
        P(),
        P(None, ("mp", "dp")),
        P(("mp", "dp")),
        P(None, ("dp", "mp"), None),
    )
    return jax.shard_map(
        per_device,
        mesh=mesh,
        in_specs=placed,
        out_specs=(
            P(None, ("dp", "mp"), None),
            P(None, ("dp", "mp"), None),
            P(),
            P(),
            P(None, "mp"),
            P("mp"),
            P("mp", None),
            P(),
            P(),
            P(),
            P(None, "mp"),
            P("mp"),
            P("mp", None),
            P(),
            P(),
            P(),
            P(),
            P(None, ("mp", "dp")),
            P(("mp", "dp")),
        ),
        check_vma=False,
    )
```

profile of v0, /device:TPU:0, one launch (start us, length us, event | category | flops | bytes accessed | tf_op | source)
XLA Modules:
  0.0 1697.0 jit_solution(3677368146295402987)
XLA Ops:
  11.9 1587.2 %while.42 = (s32[]{:T(128)}, f32[1024,768]{1,0:T(8,128)}, f32[768]{0:T(1024)}, f32[256,1024]{1,0:T(8,128)}, f32[1024,1024]{1,0:T(8,128)}, /*index=5*/f32[1024]{0...) while((s32[]{:T(128)}, f32[1024,768]{1,0:T(8,128)}, ...), condition=%wide.region_33.34_spmd.clone, body=%wide.region_0.33_spmd.clone.sunk | while | flops 22788552704 | bytes 595060224 | solution.py:288
  31.5 33.9 %all-gather.13.cloned.1.call-done = bf16[1024,1024]{1,0:T(8,128)(2,1)} async-done(((bf16[256,1024]{1,0:T(8,128)(2,1)}), bf16[1024,1024]{1,0:T(8,128)(2,1)}) %all-gather.13.cloned.1.call-update) | async-done | bytes 2097168 | tf_op jit(solution)/shard_map/while/body/eval_jaxpr/all_gather | solution.py:122
  87.9 42.1 %reduce-scatter.10.cloned.1.call-done = bf16[256,1024]{1,0:T(8,128)(2,1)} async-done(((bf16[1024,1024]{1,0:T(8,128)(2,1)}), bf16[256,1024]{1,0:T(8,128)(2,1)}) %reduce-scatter.10.cloned.1.call-update) | async-done | bytes 524304 | tf_op jit(solution)/shard_map/while/body/eval_jaxpr/reduce_scatter | solution.py:149
  137.5 42.7 %all-gather.15.cloned.1.call-done = bf16[1024,1024]{1,0:T(8,128)(2,1)} async-done(((bf16[256,1024]{1,0:T(8,128)(2,1)}), bf16[1024,1024]{1,0:T(8,128)(2,1)}) %all-gather.15.cloned.1.call-update) | async-done | bytes 2097168 | tf_op jit(solution)/shard_map/while/body/eval_jaxpr/all_gather | solution.py:160
  186.7 39.6 %all-gather.17.cloned.1.call-done = bf16[1,1024,1024]{2,1,0:T(8,128)(2,1)} async-done(((bf16[1,256,1024]{2,1,0:T(8,128)(2,1)}), bf16[1,1024,1024]{2,1,0:T(8,128)(2,1)}) %all-gather.17.cloned.1.call-update) | async-done | bytes 2097168 | tf_op jit(solution)/shard_map/while/body/eval_jaxpr/all_gather | solution.py:178
  240.4 42.7 %reduce-scatter.12.cloned.1.call-done = bf16[256,1024]{1,0:T(8,128)(2,1)} async-done(((bf16[1024,1024]{1,0:T(8,128)(2,1)}), bf16[256,1024]{1,0:T(8,128)(2,1)}) %reduce-scatter.12.cloned.1.call-update) | async-done | bytes 524304 | tf_op jit(solution)/shard_map/while/body/eval_jaxpr/reduce_scatter | solution.py:183
  308.3 26.8 %all-gather.19.cloned.1.call-done = bf16[1024,1024]{1,0:T(8,128)(2,1)} async-done(((bf16[256,1024]{1,0:T(8,128)(2,1)}), bf16[1024,1024]{1,0:T(8,128)(2,1)}) %all-gather.19.cloned.1.call-update) | async-done | bytes 2097168 | tf_op jit(solution)/shard_map/while/body/eval_jaxpr/all_gather | solution.py:191
  350.1 12.5 multiply_convert_fusion.11
  402.5 14.8 all-reduce.6
  419.2 72.0 %all-reduce.9.cloned.1.call-done = (bf16[1024,768]{1,0:T(8,128)(2,1)}, bf16[256,1024]{1,0:T(8,128)(2,1)}, bf16[1024,1024]{1,0:T(8,128)(2,1)}, bf16[1024,1024]{1,0:T(8,128)(2,1)}) async-done(((bf16[1024,768]{1,0:T(8,128)(2,1)}, bf16[256,1024]{1,0:T(8,128)(2,1)}, bf16[1024,1024]{1,0:T(8,128)(2,1)}, bf16[1024,1024]{1,0:T(8,128)(2,1)}), (bf16[1024,768]{1,0:T(8,128)(2,1)}, bf16[256,1024]{1,0:T(8,128)(2,1)}, ...) | async-done | bytes 6291472 | tf_op jit(solution)/shard_map/while/body/eval_jaxpr/psum | solution.py:269
  502.6 35.0 %reduce-scatter.14.cloned.1.call-done = bf16[256,1024]{1,0:T(8,128)(2,1)} async-done(((bf16[1024,1024]{1,0:T(8,128)(2,1)}), bf16[256,1024]{1,0:T(8,128)(2,1)}) %reduce-scatter.14.cloned.1.call-update) | async-done | bytes 524304 | tf_op jit(solution)/shard_map/while/body/eval_jaxpr/reduce_scatter | solution.py:253
  560.3 32.0 %all-gather.13.cloned.1.call-done = bf16[1024,1024]{1,0:T(8,128)(2,1)} async-done(((bf16[256,1024]{1,0:T(8,128)(2,1)}), bf16[1024,1024]{1,0:T(8,128)(2,1)}) %all-gather.13.cloned.1.call-update) | async-done | bytes 2097168 | tf_op jit(solution)/shard_map/while/body/eval_jaxpr/all_gather | solution.py:122
  614.4 42.5 %reduce-scatter.10.cloned.1.call-done = bf16[256,1024]{1,0:T(8,128)(2,1)} async-done(((bf16[1024,1024]{1,0:T(8,128)(2,1)}), bf16[256,1024]{1,0:T(8,128)(2,1)}) %reduce-scatter.10.cloned.1.call-update) | async-done | bytes 524304 | tf_op jit(solution)/shard_map/while/body/eval_jaxpr/reduce_scatter | solution.py:149
  664.4 42.8 %all-gather.15.cloned.1.call-done = bf16[1024,1024]{1,0:T(8,128)(2,1)} async-done(((bf16[256,1024]{1,0:T(8,128)(2,1)}), bf16[1024,1024]{1,0:T(8,128)(2,1)}) %all-gather.15.cloned.1.call-update) | async-done | bytes 2097168 | tf_op jit(solution)/shard_map/while/body/eval_jaxpr/all_gather | solution.py:160
  713.7 39.8 %all-gather.17.cloned.1.call-done = bf16[1,1024,1024]{2,1,0:T(8,128)(2,1)} async-done(((bf16[1,256,1024]{2,1,0:T(8,128)(2,1)}), bf16[1,1024,1024]{2,1,0:T(8,128)(2,1)}) %all-gather.17.cloned.1.call-update) | async-done | bytes 2097168 | tf_op jit(solution)/shard_map/while/body/eval_jaxpr/all_gather | solution.py:178
  767.5 42.7 %reduce-scatter.12.cloned.1.call-done = bf16[256,1024]{1,0:T(8,128)(2,1)} async-done(((bf16[1024,1024]{1,0:T(8,128)(2,1)}), bf16[256,1024]{1,0:T(8,128)(2,1)}) %reduce-scatter.12.cloned.1.call-update) | async-done | bytes 524304 | tf_op jit(solution)/shard_map/while/body/eval_jaxpr/reduce_scatter | solution.py:183
  835.5 26.7 %all-gather.19.cloned.1.call-done = bf16[1024,1024]{1,0:T(8,128)(2,1)} async-done(((bf16[256,1024]{1,0:T(8,128)(2,1)}), bf16[1024,1024]{1,0:T(8,128)(2,1)}) %all-gather.19.cloned.1.call-update) | async-done | bytes 2097168 | tf_op jit(solution)/shard_map/while/body/eval_jaxpr/all_gather | solution.py:191
  929.4 14.8 all-reduce.6
  948.2 70.0 %all-reduce.9.cloned.1.call-done = (bf16[1024,768]{1,0:T(8,128)(2,1)}, bf16[256,1024]{1,0:T(8,128)(2,1)}, bf16[1024,1024]{1,0:T(8,128)(2,1)}, bf16[1024,1024]{1,0:T(8,128)(2,1)}) async-done(((bf16[1024,768]{1,0:T(8,128)(2,1)}, bf16[256,1024]{1,0:T(8,128)(2,1)}, bf16[1024,1024]{1,0:T(8,128)(2,1)}, bf16[1024,1024]{1,0:T(8,128)(2,1)}), (bf16[1024,768]{1,0:T(8,128)(2,1)}, bf16[256,1024]{1,0:T(8,128)(2,1)}, ...) | async-done | bytes 6291472 | tf_op jit(solution)/shard_map/while/body/eval_jaxpr/psum | solution.py:269
  1034.8 29.7 %reduce-scatter.14.cloned.1.call-done = bf16[256,1024]{1,0:T(8,128)(2,1)} async-done(((bf16[1024,1024]{1,0:T(8,128)(2,1)}), bf16[256,1024]{1,0:T(8,128)(2,1)}) %reduce-scatter.14.cloned.1.call-update) | async-done | bytes 524304 | tf_op jit(solution)/shard_map/while/body/eval_jaxpr/reduce_scatter | solution.py:253
  1087.4 32.0 %all-gather.13.cloned.1.call-done = bf16[1024,1024]{1,0:T(8,128)(2,1)} async-done(((bf16[256,1024]{1,0:T(8,128)(2,1)}), bf16[1024,1024]{1,0:T(8,128)(2,1)}) %all-gather.13.cloned.1.call-update) | async-done | bytes 2097168 | tf_op jit(solution)/shard_map/while/body/eval_jaxpr/all_gather | solution.py:122
  1141.5 42.5 %reduce-scatter.10.cloned.1.call-done = bf16[256,1024]{1,0:T(8,128)(2,1)} async-done(((bf16[1024,1024]{1,0:T(8,128)(2,1)}), bf16[256,1024]{1,0:T(8,128)(2,1)}) %reduce-scatter.10.cloned.1.call-update) | async-done | bytes 524304 | tf_op jit(solution)/shard_map/while/body/eval_jaxpr/reduce_scatter | solution.py:149
  1191.5 42.8 %all-gather.15.cloned.1.call-done = bf16[1024,1024]{1,0:T(8,128)(2,1)} async-done(((bf16[256,1024]{1,0:T(8,128)(2,1)}), bf16[1024,1024]{1,0:T(8,128)(2,1)}) %all-gather.15.cloned.1.call-update) | async-done | bytes 2097168 | tf_op jit(solution)/shard_map/while/body/eval_jaxpr/all_gather | solution.py:160
  1240.8 39.8 %all-gather.17.cloned.1.call-done = bf16[1,1024,1024]{2,1,0:T(8,128)(2,1)} async-done(((bf16[1,256,1024]{2,1,0:T(8,128)(2,1)}), bf16[1,1024,1024]{2,1,0:T(8,128)(2,1)}) %all-gather.17.cloned.1.call-update) | async-done | bytes 2097168 | tf_op jit(solution)/shard_map/while/body/eval_jaxpr/all_gather | solution.py:178
  1294.6 42.7 %reduce-scatter.12.cloned.1.call-done = bf16[256,1024]{1,0:T(8,128)(2,1)} async-done(((bf16[1024,1024]{1,0:T(8,128)(2,1)}), bf16[256,1024]{1,0:T(8,128)(2,1)}) %reduce-scatter.12.cloned.1.call-update) | async-done | bytes 524304 | tf_op jit(solution)/shard_map/while/body/eval_jaxpr/reduce_scatter | solution.py:183
  1362.5 26.8 %all-gather.19.cloned.1.call-done = bf16[1024,1024]{1,0:T(8,128)(2,1)} async-done(((bf16[256,1024]{1,0:T(8,128)(2,1)}), bf16[1024,1024]{1,0:T(8,128)(2,1)}) %all-gather.19.cloned.1.call-update) | async-done | bytes 2097168 | tf_op jit(solution)/shard_map/while/body/eval_jaxpr/all_gather | solution.py:191
  1404.3 12.7 multiply_convert_fusion.11
  1456.7 14.8 all-reduce.6
  1475.5 70.1 %all-reduce.9.cloned.1.call-done = (bf16[1024,768]{1,0:T(8,128)(2,1)}, bf16[256,1024]{1,0:T(8,128)(2,1)}, bf16[1024,1024]{1,0:T(8,128)(2,1)}, bf16[1024,1024]{1,0:T(8,128)(2,1)}) async-done(((bf16[1024,768]{1,0:T(8,128)(2,1)}, bf16[256,1024]{1,0:T(8,128)(2,1)}, bf16[1024,1024]{1,0:T(8,128)(2,1)}, bf16[1024,1024]{1,0:T(8,128)(2,1)}), (bf16[1024,768]{1,0:T(8,128)(2,1)}, bf16[256,1024]{1,0:T(8,128)(2,1)}, ...) | async-done | bytes 6291472 | tf_op jit(solution)/shard_map/while/body/eval_jaxpr/psum | solution.py:269
  1562.1 29.7 %reduce-scatter.14.cloned.1.call-done = bf16[256,1024]{1,0:T(8,128)(2,1)} async-done(((bf16[1024,1024]{1,0:T(8,128)(2,1)}), bf16[256,1024]{1,0:T(8,128)(2,1)}) %reduce-scatter.14.cloned.1.call-update) | async-done | bytes 524304 | tf_op jit(solution)/shard_map/while/body/eval_jaxpr/reduce_scatter | solution.py:253
  1600.8 35.3 %reduce-scatter.8.cloned.1.call-done = f32[64,10]{1,0:T(8,128)} async-done(((f32[512,10]{1,0:T(8,128)}), f32[64,10]{1,0:T(8,128)}) %reduce-scatter.8.cloned.1.call-update) | async-done | bytes 2576
  1637.2 40.9 %all-reduce.2 = (f32[1024]{0:T(1024)}, f32[1024]{0:T(1024)}, f32[1024]{0:T(1024)}, f32[1024]{0:T(1024)}, f32[1024]{0:T(1024)}, /*index=5*/f32[1024]{0:T(1024)}, f32[10,512]{1,0:T(8,128)S(1)}) all-reduce(f32[1024]{0:T(1024)} %get-tuple-element.511, f32[1024]{0:T(1024)} %get-tuple-element.512, ...), channel_id=1, replica_groups=mesh['dp'=8,'mp'=4] {'dp','mp'}, use_global_device_ids=true, to_apply=%region_34.35 | all-reduce | flops 11264 | bytes 90112 | tf_op jit(solution)/shard_map/psum | solution.py:299
  (528 shorter events, 543.0 us)
Async XLA Ops:
  11.9 53.5 %all-gather.13.cloned.1.call-start = ((), (), s32[]{:S(2)}) async-start(), calls=%async_computation.6 | async-start | bytes 2621440 | tf_op jit(solution)/shard_map/while/body/eval_jaxpr/all_gather | solution.py:122
  16.6 113.4 %reduce-scatter.10.cloned.1.call-start = ((), (), s32[]{:S(2)}) async-start(), calls=%async_computation.7 | async-start | bytes 2621440 | tf_op jit(solution)/shard_map/while/body/eval_jaxpr/reduce_scatter | solution.py:149
  28.7 308.9 %copy-start.14 = (bf16[10,4,2,64]{3,0,1,2:T(8,128)(2,1)}, bf16[10,4,2,64]{3,0,1,2:T(8,128)(2,1)S(1)}, u32[]{:S(2)}) copy-start(bf16[10,4,2,64]{3,0,1,2:T(8,128)(2,1)S(1)} %copy.85) | copy-start | bytes 30724 | tf_op jit(solution)/shard_map/while
  87.2 93.0 %all-gather.15.cloned.1.call-start = ((), (), s32[]{:S(2)}) async-start(), calls=%async_computation.8 | async-start | bytes 2621440 | tf_op jit(solution)/shard_map/while/body/eval_jaxpr/all_gather | solution.py:160
  134.8 91.5 %all-gather.17.cloned.1.call-start = ((), (), s32[]{:S(2)}) async-start(), calls=%async_computation.9 | async-start | bytes 2621440 | tf_op jit(solution)/shard_map/while/body/eval_jaxpr/all_gather | solution.py:178
  137.5 145.7 %reduce-scatter.12.cloned.1.call-start = ((), (), s32[]{:S(2)}) async-start(), calls=%async_computation.10 | async-start | bytes 2621440 | tf_op jit(solution)/shard_map/while/body/eval_jaxpr/reduce_scatter | solution.py:183
  240.4 94.7 %all-gather.19.cloned.1.call-start = ((), (), s32[]{:S(2)}) async-start(), calls=%async_computation.11 | async-start | bytes 2621440 | tf_op jit(solution)/shard_map/while/body/eval_jaxpr/all_gather | solution.py:191
  289.7 107.2 %reduce-scatter.16.cloned.1.call-start = ((), (), s32[]{:S(2)}) async-start(), calls=%async_computation.14 | async-start | bytes 2621440 | tf_op jit(solution)/shard_map/while/body/eval_jaxpr/reduce_scatter | solution.py:168
  296.9 194.3 %all-reduce.9.cloned.1.call-start = ((), (), s32[]{:S(2)}) async-start(), calls=%async_computation.12 | async-start | bytes 12582912 | tf_op jit(solution)/shard_map/while/body/eval_jaxpr/psum | solution.py:269
  387.5 150.1 %reduce-scatter.14.cloned.1.call-start = ((), (), s32[]{:S(2)}) async-start(), calls=%async_computation.13 | async-start | bytes 2621440 | tf_op jit(solution)/shard_map/while/body/eval_jaxpr/reduce_scatter | solution.py:253
  542.1 50.2 %all-gather.13.cloned.1.call-start = ((), (), s32[]{:S(2)}) async-start(), calls=%async_computation.6 | async-start | bytes 2621440 | tf_op jit(solution)/shard_map/while/body/eval_jaxpr/all_gather | solution.py:122
  546.9 110.0 %reduce-scatter.10.cloned.1.call-start = ((), (), s32[]{:S(2)}) async-start(), calls=%async_computation.7 | async-start | bytes 2621440 | tf_op jit(solution)/shard_map/while/body/eval_jaxpr/reduce_scatter | solution.py:149
  557.5 307.2 %copy-start.14 = (bf16[10,4,2,64]{3,0,1,2:T(8,128)(2,1)}, bf16[10,4,2,64]{3,0,1,2:T(8,128)(2,1)S(1)}, u32[]{:S(2)}) copy-start(bf16[10,4,2,64]{3,0,1,2:T(8,128)(2,1)S(1)} %copy.85) | copy-start | bytes 30724 | tf_op jit(solution)/shard_map/while
  614.1 93.1 %all-gather.15.cloned.1.call-start = ((), (), s32[]{:S(2)}) async-start(), calls=%async_computation.8 | async-start | bytes 2621440 | tf_op jit(solution)/shard_map/while/body/eval_jaxpr/all_gather | solution.py:160
  661.8 91.7 %all-gather.17.cloned.1.call-start = ((), (), s32[]{:S(2)}) async-start(), calls=%async_computation.9 | async-start | bytes 2621440 | tf_op jit(solution)/shard_map/while/body/eval_jaxpr/all_gather | solution.py:178
  664.4 145.8 %reduce-scatter.12.cloned.1.call-start = ((), (), s32[]{:S(2)}) async-start(), calls=%async_computation.10 | async-start | bytes 2621440 | tf_op jit(solution)/shard_map/while/body/eval_jaxpr/reduce_scatter | solution.py:183
  767.5 94.7 %all-gather.19.cloned.1.call-start = ((), (), s32[]{:S(2)}) async-start(), calls=%async_computation.11 | async-start | bytes 2621440 | tf_op jit(solution)/shard_map/while/body/eval_jaxpr/all_gather | solution.py:191
  816.7 107.0 %reduce-scatter.16.cloned.1.call-start = ((), (), s32[]{:S(2)}) async-start(), calls=%async_computation.14 | async-start | bytes 2621440 | tf_op jit(solution)/shard_map/while/body/eval_jaxpr/reduce_scatter | solution.py:168
  824.2 194.0 %all-reduce.9.cloned.1.call-start = ((), (), s32[]{:S(2)}) async-start(), calls=%async_computation.12 | async-start | bytes 12582912 | tf_op jit(solution)/shard_map/while/body/eval_jaxpr/psum | solution.py:269
  914.5 150.0 %reduce-scatter.14.cloned.1.call-start = ((), (), s32[]{:S(2)}) async-start(), calls=%async_computation.13 | async-start | bytes 2621440 | tf_op jit(solution)/shard_map/while/body/eval_jaxpr/reduce_scatter | solution.py:253
  1069.3 50.2 %all-gather.13.cloned.1.call-start = ((), (), s32[]{:S(2)}) async-start(), calls=%async_computation.6 | async-start | bytes 2621440 | tf_op jit(solution)/shard_map/while/body/eval_jaxpr/all_gather | solution.py:122
  1074.0 109.9 %reduce-scatter.10.cloned.1.call-start = ((), (), s32[]{:S(2)}) async-start(), calls=%async_computation.7 | async-start | bytes 2621440 | tf_op jit(solution)/shard_map/while/body/eval_jaxpr/reduce_scatter | solution.py:149
  1084.7 307.2 %copy-start.14 = (bf16[10,4,2,64]{3,0,1,2:T(8,128)(2,1)}, bf16[10,4,2,64]{3,0,1,2:T(8,128)(2,1)S(1)}, u32[]{:S(2)}) copy-start(bf16[10,4,2,64]{3,0,1,2:T(8,128)(2,1)S(1)} %copy.85) | copy-start | bytes 30724 | tf_op jit(solution)/shard_map/while
  1141.3 93.0 %all-gather.15.cloned.1.call-start = ((), (), s32[]{:S(2)}) async-start(), calls=%async_computation.8 | async-start | bytes 2621440 | tf_op jit(solution)/shard_map/while/body/eval_jaxpr/all_gather | solution.py:160
  1188.9 91.7 %all-gather.17.cloned.1.call-start = ((), (), s32[]{:S(2)}) async-start(), calls=%async_computation.9 | async-start | bytes 2621440 | tf_op jit(solution)/shard_map/while/body/eval_jaxpr/all_gather | solution.py:178
  1191.5 145.8 %reduce-scatter.12.cloned.1.call-start = ((), (), s32[]{:S(2)}) async-start(), calls=%async_computation.10 | async-start | bytes 2621440 | tf_op jit(solution)/shard_map/while/body/eval_jaxpr/reduce_scatter | solution.py:183
  1294.6 94.7 %all-gather.19.cloned.1.call-start = ((), (), s32[]{:S(2)}) async-start(), calls=%async_computation.11 | async-start | bytes 2621440 | tf_op jit(solution)/shard_map/while/body/eval_jaxpr/all_gather | solution.py:191
  1343.9 107.2 %reduce-scatter.16.cloned.1.call-start = ((), (), s32[]{:S(2)}) async-start(), calls=%async_computation.14 | async-start | bytes 2621440 | tf_op jit(solution)/shard_map/while/body/eval_jaxpr/reduce_scatter | solution.py:168
  1351.2 194.4 %all-reduce.9.cloned.1.call-start = ((), (), s32[]{:S(2)}) async-start(), calls=%async_computation.12 | async-start | bytes 12582912 | tf_op jit(solution)/shard_map/while/body/eval_jaxpr/psum | solution.py:269
  1441.8 150.0 %reduce-scatter.14.cloned.1.call-start = ((), (), s32[]{:S(2)}) async-start(), calls=%async_computation.13 | async-start | bytes 2621440 | tf_op jit(solution)/shard_map/while/body/eval_jaxpr/reduce_scatter | solution.py:253
  1599.1 37.0 %reduce-scatter.8.cloned.1.call-start = ((), (), s32[]{:S(2)}) async-start(), calls=%async_computation.5 | async-start | bytes 294912
  1599.1 89.3 %copy-start.18 = (f32[10,512]{1,0:T(8,128)S(1)}, f32[10,512]{1,0:T(8,128)}, u32[]{:S(2)}) copy-start(f32[10,512]{1,0:T(8,128)} %copy-done.17) | copy-start | bytes 61444
  (102 other events, 1953.8 us)
Sparse Core Ops, SparseCore 0:
  16.7 48.6 all-gather.12
  87.3 42.5 reduce-scatter.9
  135.0 45.2 all-gather.14
  181.7 44.6 all-gather.16
  240.5 42.5 reduce-scatter.11
  289.8 45.2 all-gather.18
  337.5 42.5 reduce-scatter.15
  387.6 103.5 all-reduce.8
  493.6 43.9 reduce-scatter.13
  547.0 45.2 all-gather.12
  614.2 42.6 reduce-scatter.9
  661.9 45.2 all-gather.14
  708.7 44.6 all-gather.16
  767.6 42.5 reduce-scatter.11
  816.9 45.2 all-gather.18
  864.4 42.5 reduce-scatter.15
  914.6 103.5 all-reduce.8
  1020.5 43.9 reduce-scatter.13
  1074.2 45.2 all-gather.12
  1141.4 42.5 reduce-scatter.9
  1189.0 45.2 all-gather.14
  1235.9 44.6 all-gather.16
  1294.7 42.5 reduce-scatter.11
  1344.0 45.2 all-gather.18
  1391.7 42.5 reduce-scatter.15
  1442.0 103.5 all-reduce.8
  1547.8 43.9 reduce-scatter.13
Sparse Core Ops, SparseCore 1:
  1603.1 32.9 reduce-scatter.7
where the time goes:
time: 1700 us
  waiting for transfers between devices  1020 us (60%)
  matrix products  305 us (18%)
  other arithmetic  202 us (12%)
  blocking collectives  114 us (7%)
  local copies, waits for them, and re-layouts  27.9 us (2%)
    psum x3, waiting for transfers between devices, micro_step(): lax.psum(grad_qkv.astype(jnp.bfloat16), 'dp').astype(jnp.float32)  212 us
    all_gather x3, waiting for transfers between devices, micro_step(): lax.all_gather((hat_second * ln2_gain + ln2_bias).astype(jnp.bfloat16), '...  128 us
    reduce_scatter x3, waiting for transfers between devices, micro_step(): lax.psum_scatter(product_transposed(d_up, up_weight).astype(jnp.bfloat16)...  128 us
    reduce_scatter x3, waiting for transfers between devices, micro_step(): lax.psum_scatter(jnp.dot(head_rows, out_weight, preferred_element_type=jn...  127 us
    all_gather x3, waiting for transfers between devices, micro_step(): cot_full = lax.all_gather(cotangent_mb, 'mp', axis=0, tiled=True)  119 us
    all_gather x3, waiting for transfers between devices, micro_step(): lax.all_gather((hat_first * ln1_gain + ln1_bias).astype(jnp.bfloat16), 'm...  97.8 us
    reduce_scatter x3, waiting for transfers between devices, micro_step(): lax.psum_scatter(product_transposed(d_qkv, qkv_weight).astype(jnp.bfloat1...  94.3 us
    all_gather x3, waiting for transfers between devices, micro_step(): lax.all_gather(d_resid.astype(jnp.bfloat16), 'mp', axis=0, tiled=True)  80.3 us
  transfers between devices with their start and end apart: 28, of which 25 were waited for; matrix products, arithmetic and copies ran while one was open for 21% of the time, Pallas kernels for 0%

commit v1 on v0

--- a/solution.py
+++ b/solution.py
@@ -1,8 +1,11 @@
+import functools
 import math
 
 import jax
 import jax.numpy as jnp
 from jax import lax
+from jax.experimental import pallas as pl
+from jax.experimental.pallas import tpu as pltpu
 from jax.sharding import PartitionSpec as P
 
 HEAD_DIM = 64
@@ -335,54 +338,1569 @@
     )
 
 
+ALL = ("pl", "core", "mp")
+QB = 256
+MICRO = 3
+
+
+def nt(left, right):
+    return lax.dot_general(
+        left, right, (((1,), (1,)), ((), ())), preferred_element_type=jnp.float32
+    )
+
+
+def nn(left, right):
+    return jnp.dot(left, right, preferred_element_type=jnp.float32)
+
+
+def half_mask(value, head):
+    lane = lax.broadcasted_iota(jnp.int32, value.shape, 1)
+    keep = (lane < HEAD_DIM) if head == 0 else (lane >= HEAD_DIM)
+    return jnp.where(keep, value, jnp.zeros_like(value))
+
+
+GELU_A = math.sqrt(2.0 / math.pi)
+GELU_B = 0.044715
+
+
+def feed_kernel(
+    heads_ref, tokens_ref, cot_ref, out_own_ref, out_ref, vectors_ref,
+    own_up_ref, own_down_ref, weight_ref, bias_ref,
+    block_ref, resid_ref, dheads_ref, gout_ref, sums_ref, grad_ref, gbias_ref,
+    heads_s, normed_s, resid_s, mlp_s, dn_s,
+):
+    step = pl.program_id(0)
+    blocks, near, cores, share, lanes = heads_ref.shape
+    own_rows = out_own_ref.shape[0]
+    out_bias, gain, offset, down_bias = [vectors_ref[j : j + 1] for j in range(4)]
+
+    @pl.when(step == 0)
+    def _before():
+        for m in range(blocks):
+            rows = slice(m * share, (m + 1) * share)
+            heads = jnp.concatenate(
+                [heads_ref[m, r, c] for r in range(near) for c in range(cores)], 1
+            )
+            heads_s[rows] = heads
+            resid = (
+                tokens_ref[rows].astype(jnp.float32)
+                + nn(heads[:, :own_rows], out_own_ref[...])
+                + nn(heads[:, own_rows:], out_ref[...])
+                + out_bias
+            )
+            resid_s[rows] = resid
+            hat, _ = normalize(resid)
+            normed_s[rows] = (hat * gain + offset).astype(jnp.bfloat16)
+
+    normed, cot = normed_s[...], cot_ref[...]
+    groups, depth, width = grad_ref.shape[1:]
+    half_rows = depth // 2
+    units = (groups - 1) * half_rows
+    up = jnp.concatenate(
+        [jnp.transpose(own_up_ref[...]), weight_ref[0, :, :half_rows].reshape(units, width)], 0
+    )
+    down = jnp.concatenate(
+        [own_down_ref[0], weight_ref[0, :, half_rows:].reshape(units, width)], 0
+    )
+    act = nt(normed, up) + bias_ref[0]
+    square = act * act
+    curve = jnp.tanh(GELU_A * act * (1.0 + GELU_B * square))
+    half = 0.5 * (1.0 + curve)
+    hidden = (act * half).astype(jnp.bfloat16)
+    slope = half + 0.5 * act * (1.0 - curve * curve) * (
+        GELU_A * (1.0 + (3.0 * GELU_B) * square)
+    )
+    d_act = nt(cot, down) * slope
+    gbias_ref[0] = jnp.sum(d_act, 0, keepdims=True)
+    d_low = d_act.astype(jnp.bfloat16)
+    gup = outer_sum(d_low, normed).astype(jnp.bfloat16)
+    gdown = outer_sum(hidden, cot).astype(jnp.bfloat16)
+    grad_ref[0, :, :half_rows] = gup.reshape(groups, half_rows, width)
+    grad_ref[0, :, half_rows:] = gdown.reshape(groups, half_rows, width)
+    mlp, dn = nn(hidden, down), nn(d_low, up)
+
+    @pl.when(step == 0)
+    def _first():
+        mlp_s[...] = mlp
+        dn_s[...] = dn
+
+    @pl.when(step > 0)
+    def _later():
+        mlp_s[...] += mlp
+        dn_s[...] += dn
+
+    @pl.when(step == pl.num_programs(0) - 1)
+    def _after():
+        sums = [jnp.zeros((1, width), jnp.float32) for _ in range(4)]
+        for m in range(blocks):
+            rows = slice(m * share, (m + 1) * share)
+            resid, d_second = resid_s[rows], dn_s[rows]
+            block_ref[rows] = (resid + mlp_s[rows] + down_bias).astype(jnp.bfloat16)
+            hat, inverse = normalize(resid)
+            cot_wide = cot_ref[rows].astype(jnp.float32)
+            d_resid = cot_wide + norm_back(d_second, hat, inverse, gain)
+            resid_ref[rows] = d_resid
+            for j, value in enumerate((d_second * hat, d_second, d_resid, cot_wide)):
+                sums[j] = sums[j] + jnp.sum(value, 0, keepdims=True)
+            d_attn = d_resid.astype(jnp.bfloat16)
+            normed_s[rows] = d_attn
+            d_own = nt(d_attn, out_own_ref[...]).astype(jnp.bfloat16)
+            d_rest = nt(d_attn, out_ref[...]).astype(jnp.bfloat16)
+            for r in range(near):
+                for c in range(cores):
+                    source = d_rest if r else d_own
+                    at = (2 * r + c) * lanes - (own_rows if r else 0)
+                    dheads_ref[m, r, c] = source[:, at : at + lanes]
+        for j in range(4):
+            sums_ref[j : j + 1] = sums[j]
+        for j in range(near):
+            columns = slice(j * own_rows, (j + 1) * own_rows)
+            gout_ref[columns] = outer_sum(heads_s[:, columns], normed_s[...]).astype(jnp.bfloat16)
+
+
+def feed_forward(heads, tokens, cot, out_own, out, vectors, own_up, own_down, weights, bias):
+    rows, width = tokens.shape
+    tiles, others, depth, _ = weights.shape
+    groups = others + 1
+    units = groups * depth // 2
+    once = pl.Buffered(1)
+
+    def whole(shape):
+        return pl.BlockSpec(shape, lambda i: (0,) * len(shape), pipeline_mode=once)
+
+    shaped, bf16, f32 = jax.ShapeDtypeStruct, jnp.bfloat16, jnp.float32
+    line = pl.BlockSpec((1, 1, units), lambda i: (i, 0, 0))
+    square = (rows, width)
+    return pl.pallas_call(
+        feed_kernel,
+        grid=(tiles,),
+        in_specs=[
+            whole(heads.shape),
+            whole(square),
+            whole(square),
+            whole(out_own.shape),
+            whole(out.shape),
+            whole(vectors.shape),
+            pl.BlockSpec((width, depth // 2), lambda i: (0, i)),
+            pl.BlockSpec((1, depth // 2, width), lambda i: (i, 0, 0)),
+            pl.BlockSpec((1, others, depth, width), lambda i: (i, 0, 0, 0)),
+            line,
+        ],
+        out_specs=[
+            whole(square),
+            whole(square),
+            whole(heads.shape),
+            whole((width, width)),
+            whole((4, width)),
+            pl.BlockSpec((1, groups, depth, width), lambda i: (i, 0, 0, 0)),
+            line,
+        ],
+        out_shape=[
+            shaped(square, bf16),
+            shaped(square, f32),
+            shaped(heads.shape, bf16),
+            shaped((width, width), bf16),
+            shaped((4, width), f32),
+            shaped((tiles, groups, depth, width), bf16),
+            shaped((tiles, 1, units), f32),
+        ],
+        scratch_shapes=[
+            pltpu.VMEM(square, bf16),
+            pltpu.VMEM(square, bf16),
+            pltpu.VMEM(square, f32),
+            pltpu.VMEM(square, f32),
+            pltpu.VMEM(square, f32),
+        ],
+        compiler_params=pltpu.CompilerParams(vmem_limit_bytes=62 << 20),
+        cost_estimate=pl.CostEstimate(
+            flops=12 * rows * width * tiles * units, bytes_accessed=60_000_000,
+            transcendentals=rows * tiles * units,
+        ),
+        name="feed_forward",
+    )(heads, tokens, cot, out_own, out, vectors, own_up, own_down, weights, bias)
+
+
+MESH_IDS = pl.DeviceIdType.MESH
+
+
+def position():
+    return lax.axis_index("pl"), lax.axis_index("core"), lax.axis_index("mp")
+
+
+def plane_at(plane, offset):
+    across, down = lax.rem(plane, 2), lax.div(plane, 2)
+    if offset & 1:
+        across = 1 - across
+    if offset & 2:
+        down = 1 - down
+    return 2 * down + across
+
+
+def greet(partners):
+    barrier = pltpu.get_barrier_semaphore()
+    for partner in partners:
+        pl.semaphore_signal(barrier, inc=1, device_id=partner, device_id_type=MESH_IDS)
+    pl.semaphore_wait(barrier, len(partners))
+
+
+def column_partners():
+    plane, core, zed = position()
+    found = [(plane, core, lax.rem(zed + step, 4)) for step in range(1, 4)]
+    return found + [(plane, 1 - core, lax.rem(zed + step, 4)) for step in range(4)]
+
+
+def plane_partners():
+    plane, core, zed = position()
+    return [(plane_at(plane, offset), core, zed) for offset in range(1, 4)]
+
+
+class Wires:
+    def __init__(self, sends, recvs):
+        self.sends, self.recvs, self.out = sends, recvs, []
+
+    def copy(self, source, target, slot, device):
+        return pltpu.make_async_remote_copy(
+            src_ref=source,
+            dst_ref=target,
+            send_sem=self.sends.at[slot],
+            recv_sem=self.recvs.at[slot],
+            device_id=device,
+            device_id_type=MESH_IDS,
+        )
+
+    def put(self, source, target, slot, device):
+        copy = self.copy(source, target, slot, device)
+        copy.start()
+        self.out.append((copy, None))
+
+    def put_unless(self, own, source, target, slot, device):
+        copy = self.copy(source, target, slot, device)
+
+        @pl.when(own)
+        def _here():
+            pltpu.make_async_copy(source, target, self.recvs.at[slot]).start()
+
+        @pl.when(jnp.logical_not(own))
+        def _there():
+            copy.start()
+
+        self.out.append((copy, own))
+
+    def put_if(self, valid, source, target, slot, device):
+        copy = self.copy(source, target, slot, device)
+        pl.when(valid)(copy.start)
+        self.out.append((copy, jnp.logical_not(valid)))
+
+    def got(self, target, slot, device):
+        self.copy(target, target, slot, device).wait_recv()
+
+    def got_if(self, valid, target, slot, device):
+        pl.when(valid)(self.copy(target, target, slot, device).wait_recv)
+
+    def wait_sent(self, puts):
+        gone = [id(put) for put in puts]
+        self.out = [put for put in self.out if id(put) not in gone]
+        for copy, own in puts:
+            if own is None:
+                copy.wait_send()
+            else:
+                pl.when(jnp.logical_not(own))(copy.wait_send)
+
+    def finish(self):
+        self.wait_sent(list(self.out))
+
+
+ANYWHERE = pl.BlockSpec(memory_space=pl.ANY)
+
+
+def visible_to(seg_col, seg_row, block):
+    keys = (block + 1) * QB
+    lanes = seg_row[:, block * QB : keys]
+    cols = seg_col[:keys, :]
+    same = jnp.concatenate([cols, cols], 1) == lanes
+    rows = lax.broadcasted_iota(jnp.int32, (keys, QB), 0)
+    places = lax.broadcasted_iota(jnp.int32, (keys, QB), 1) + block * QB
+    return same & (rows <= places)
+
+
+def forward_pair(slots, qkv, keys_pre, values_pre, seg_row, seg_col, heads, logs):
+    seq = qkv.shape[0]
+    keys = qkv[:, 128:256]
+    values_t = jnp.transpose(qkv[:, 256:384])
+    values_pre_t = jnp.transpose(values_pre)
+    pre_row = lax.broadcasted_iota(jnp.int32, (keys_pre.shape[0], QB), 0)
+    for block in range(seq // QB):
+        extent = (block + 1) * QB
+        here = slice(block * QB, extent)
+        visible = visible_to(seg_col, seg_row, block)
+        queries = qkv[here, :128] * 0.125
+        parts = []
+        for head in range(2):
+            rows = slice(head * HEAD_DIM, (head + 1) * HEAD_DIM)
+            query = half_mask(queries, head)
+            s_tok = jnp.where(visible, nt(keys[:extent], query), MASKED)
+            s_pre = jnp.where(pre_row < slots, nt(keys_pre, query), MASKED)
+            top = jnp.maximum(
+                jnp.max(s_tok, 0, keepdims=True), jnp.max(s_pre, 0, keepdims=True)
+            )
+            p_tok, p_pre = jnp.exp(s_tok - top), jnp.exp(s_pre - top)
+            total = jnp.sum(p_tok, 0, keepdims=True) + jnp.sum(p_pre, 0, keepdims=True)
+            mixed = nn(values_t[rows, :extent], p_tok.astype(jnp.bfloat16)) + nn(
+                values_pre_t[rows], p_pre.astype(jnp.bfloat16)
+            )
+            parts.append(mixed * (1.0 / total))
+            logs[head : head + 1, here] = top + jnp.log(total)
+        heads[here, :] = jnp.transpose(jnp.concatenate(parts, 0)).astype(jnp.bfloat16)
+
+
+PAIRS = 6
+
+
+def front_kernel(
+    slots,
+    normed_ref, qkv_ref, bias_ref, table_ref, ids_ref, own_ref,
+    rows_out, weight_out, qkv_out, heads_out, feed_out, proj_out,
+    log_out, tab_out, seg_out, live_out, bias_out,
+    sends, recvs, local,
+    rows_v, weight_v, qkv_v, heads_v, log_v, biases_v, tables_v, ids_v, other_v, col_v, feed_v,
+):
+    plane, core, zed = position()
+    parity = lax.rem(zed, 2)
+    mine = 2 * parity + core
+    origin = lax.div(zed, 2)
+    sibling = (plane, 1 - core, zed)
+    share = normed_ref.shape[1]
+    seq = 4 * share
+    around = [(plane_at(plane, offset), core, zed) for offset in range(4)]
+    ahead = [lax.rem(zed + step, 4) for step in range(4)]
+    greet(column_partners() + plane_partners())
+    wires = Wires(sends, recvs)
+    slot_at = {}
+
+    def slot(*name):
+        return slot_at.setdefault(name, len(slot_at))
+
+    width = qkv_ref.shape[0] // 4
+
+    def strip(at):
+        return pl.ds(pl.multiple_of(at * width, 32), width)
+
+    def rolled(z_from, z_at):
+        return lax.rem(z_from + 2 * lax.rem(z_at, 2), 4)
+
+    def apart(z_of, z_at):
+        return lax.rem(z_of - z_at + 4, 4)
+
+    own_copies = [
+        pltpu.make_async_copy(qkv_ref, weight_v.at[rolled(zed, zed)], local.at[0]),
+        pltpu.make_async_copy(bias_ref, biases_v.at[zed], local.at[1]),
+        pltpu.make_async_copy(table_ref, tables_v.at[plane, core, zed], local.at[2]),
+        pltpu.make_async_copy(ids_ref, ids_v, local.at[3]),
+    ]
+    for copy in own_copies:
+        copy.start()
+    wires.put(ids_ref, other_v, slot("ids"), sibling)
+
+    sides = (1, -1)
+    hops = [(sign, hop) for hop in range(1, 4) for sign in sides]
+
+    def owner(sign, hop):
+        at = zed - sign * hop
+        return lax.rem(at + 4, 4), jnp.logical_and(at >= 0, at <= 3)
+
+    def next_along(sign):
+        at = zed + sign
+        return lax.rem(at + 4, 4), jnp.logical_and(at >= 0, at <= 3)
+
+    def early_parts(z_of, z_at):
+        return (
+            weight_v.at[rolled(z_of, z_at), strip(plane)],
+            biases_v.at[z_of],
+            tables_v.at[plane, core, z_of],
+        )
+
+    def late_part(at, core_at, z_of, z_at):
+        return feed_v.at[at, core_at, apart(z_of, z_at) - 1]
+
+    total = own_ref.shape[0]
+    part_rows = feed_out.shape[3] // 2
+    halves = (pl.ds(0, total // 2), pl.ds(total // 2, total // 2))
+    routes = ((1, 2), (2, 1))
+
+    def half_strip(at, half):
+        return pl.ds(pl.multiple_of(at * width + half * (width // 2), 16), width // 2)
+
+    def send_early(sign, hop):
+        z_of, there_is = owner(sign, hop - 1)
+        z_to, can = next_along(sign)
+        valid = jnp.logical_and(there_is, can)
+        sources, targets = early_parts(z_of, zed), early_parts(z_of, z_to)
+        for kind in range(3):
+            wires.put_if(
+                valid, sources[kind], targets[kind], slot("e", sign, hop, kind), (plane, core, z_to)
+            )
+
+    def send_late(sign, hop):
+        z_of, there_is = owner(sign, hop - 1)
+        z_to, can = next_along(sign)
+        valid = jnp.logical_and(there_is, can)
+        source = own_ref if hop == 1 else late_part(plane, core, z_of, zed)
+        wires.put_if(
+            valid, source, late_part(plane, core, z_of, z_to), slot("l", sign, hop), (plane, core, z_to)
+        )
+
+    def take_early(sign, hop):
+        z_of, valid = owner(sign, hop)
+        back = (plane, core, lax.rem(zed + 4 - sign, 4))
+        for kind, part in enumerate(early_parts(z_of, zed)):
+            wires.got_if(valid, part, slot("e", sign, hop, kind), back)
+        if hop < 3:
+            send_early(sign, hop + 1)
+        for half in range(2):
+            part = weight_v.at[rolled(z_of, zed), half_strip(plane, half)]
+            for offset in routes[half]:
+                wires.put_if(valid, part, part, slot("ep", sign, hop, half, offset), around[offset])
+
+    def early_across(sign, hop):
+        z_of, valid = owner(sign, hop)
+        for half, (came, goes) in enumerate(routes):
+            part = weight_v.at[rolled(z_of, zed), half_strip(plane_at(plane, came), half)]
+            wires.got_if(valid, part, slot("ep", sign, hop, half, came), around[came])
+            wires.put_if(valid, part, part, slot("ep", sign, hop, half, 3), around[goes])
+
+    def early_end(sign, hop):
+        z_of, valid = owner(sign, hop)
+        for half, (came, goes) in enumerate(routes):
+            for offset, over in ((goes, goes), (3, goes)):
+                part = weight_v.at[rolled(z_of, zed), half_strip(plane_at(plane, offset), half)]
+                wires.got_if(valid, part, slot("ep", sign, hop, half, offset), around[over])
+
+    def take_late(sign, hop):
+        z_of, valid = owner(sign, hop)
+        part = late_part(plane, core, z_of, zed)
+        wires.got_if(valid, part, slot("l", sign, hop), (plane, core, lax.rem(zed + 4 - sign, 4)))
+        if hop < 3:
+            send_late(sign, hop + 1)
+        for half in range(2):
+            piece = part.at[halves[half]]
+            for offset in routes[half]:
+                wires.put_if(
+                    valid, piece, piece, slot("lp", sign, hop, half, offset), around[offset]
+                )
+        wires.put_if(valid, part, part, slot("ls", sign, hop, 0), sibling)
+
+    def take_across(sign, hop):
+        z_of, valid = owner(sign, hop)
+        for half, (came, goes) in enumerate(routes):
+            piece = late_part(plane_at(plane, came), core, z_of, zed).at[halves[half]]
+            wires.got_if(valid, piece, slot("lp", sign, hop, half, came), around[came])
+            wires.put_if(valid, piece, piece, slot("lp", sign, hop, half, 3), around[goes])
+        for half, (_, other) in enumerate(routes):
+            piece = late_part(plane_at(plane, other), core, z_of, zed).at[halves[half]]
+            wires.got_if(valid, piece, slot("lp", sign, hop, half, other), around[other])
+        for offset in (1, 2):
+            part = late_part(plane_at(plane, offset), core, z_of, zed)
+            wires.put_if(valid, part, part, slot("ls", sign, hop, offset), sibling)
+
+    def take_far(sign, hop):
+        z_of, valid = owner(sign, hop)
+        part = late_part(plane_at(plane, 3), core, z_of, zed)
+        for half, (_, goes) in enumerate(routes):
+            wires.got_if(
+                valid, part.at[halves[half]], slot("lp", sign, hop, half, 3), around[goes]
+            )
+        wires.put_if(valid, part, part, slot("ls", sign, hop, 3), sibling)
+
+    def end_across(sign, hop):
+        z_of, valid = owner(sign, hop)
+        for offset in range(4):
+            part = late_part(plane_at(plane, offset), 1 - core, z_of, zed)
+            wires.got_if(valid, part, slot("ls", sign, hop, offset), sibling)
+
+    for copy in own_copies:
+        copy.wait()
+    for sign in sides:
+        send_early(sign, 1)
+    first_far = slot("nb", 0)
+    slot("nb", 1)
+    first_row = slot("n", 0)
+    for step in range(1, 4):
+        slot("n", step)
+    outside = lax.div(zed, 2) != core
+    near_home = jnp.logical_or(zed == 1, zed == 2)
+    far_z = zed + 1 - 2 * parity
+    first_over = slot("f", 0)
+    for step in range(1, 4):
+        slot("f", step)
+
+    def send_rows(kind):
+        for half in range(2):
+            k = 2 * half + kind
+            z_to = 2 * core + half
+            own = jnp.logical_and(core == kind, z_to == zed)
+            source, target = normed_ref.at[1 if kind else k], rows_v.at[kind, zed]
+            number = first_row + lax.rem(k + 4 - zed, 4)
+
+            @pl.when(own)
+            def _here():
+                pltpu.make_async_copy(source, target, recvs.at[number]).start()
+
+            goes = jnp.logical_not(own)
+            if kind:
+                far_to = jnp.logical_or(z_to == 0, z_to == 3)
+                goes = jnp.logical_and(goes, jnp.logical_not(jnp.logical_and(outside, far_to)))
+            wires.put_if(goes, source, target, number, (plane, kind, z_to))
+
+    def pass_rows(kind):
+        here = core == kind
+        for step in range(4):
+            z_from = lax.rem(2 * parity + kind + 4 - step, 4)
+            block = rows_v.at[kind, z_from]
+            if kind:
+                from_outside = jnp.logical_and(here, lax.div(z_from, 2) != origin)
+                via = jnp.logical_and(from_outside, jnp.logical_not(near_home))
+                far_number = first_far + lax.rem(z_from, 2)
+                wires.got_if(via, block, far_number, sibling)
+                wires.got_if(
+                    jnp.logical_and(here, jnp.logical_not(via)), block, first_row + step, sibling
+                )
+                wires.put_if(
+                    jnp.logical_and(from_outside, near_home),
+                    block,
+                    block,
+                    far_number,
+                    (plane, core, far_z),
+                )
+            else:
+                wires.got_if(here, block, first_row + step, sibling)
+            wires.put_if(here, block, block, first_over + step, sibling)
+
+    def rows_passed(kind):
+        for step in range(4):
+            z_from = lax.rem(2 * parity + kind + 4 - step, 4)
+            wires.got_if(core != kind, rows_v.at[kind, z_from], first_over + step, sibling)
+
+    send_rows(0)
+    for sign in sides:
+        send_late(sign, 1)
+    for hop in range(1, 4):
+        for sign in sides:
+            take_early(sign, hop)
+    for sign in sides:
+        take_late(sign, 1)
+    for sign, hop in hops:
+        early_across(sign, hop)
+    pass_rows(0)
+    send_rows(1)
+    for offset in range(1, 4):
+        wires.put(
+            tables_v.at[plane, core], tables_v.at[plane, core], slot("tp", offset), around[offset]
+        )
+    for offset in range(1, 4):
+        wires.got(tables_v.at[plane_at(plane, offset), core], slot("tp", offset), around[offset])
+    wires.put(tables_v.at[:, core], tables_v.at[:, core], slot("ts"), sibling)
+
+    wires.got(other_v, slot("ids"), sibling)
+    wires.got(tables_v.at[:, 1 - core], slot("ts"), sibling)
+    for row in range(2):
+        at = 1 if row else 2 * parity
+        here = jnp.where(origin == core, ids_v[at], other_v[at])
+        seg = here[:, :seq]
+        length = jnp.concatenate([here[:, seq:]] * (seq // 128), 1)
+        live = (lax.broadcasted_iota(jnp.int32, (1, seq), 1) < length).astype(jnp.int32)
+        seg_out[row] = seg
+        live_out[row] = live
+        line = jnp.where(live > 0, seg, -1).astype(jnp.float32)
+        col_v[row] = jnp.transpose(jnp.broadcast_to(line, (128, seq)))
+    for at in range(8):
+        for step in range(4):
+            bias_out[at, step : step + 1] = biases_v[ahead[step], 2, at : at + 1]
+    for at in range(4):
+        z_at = rolled(at, zed)
+        for s in range(2):
+            tab_out[at, :, 128 * s : 128 * s + 128] = jnp.concatenate(
+                [tables_v[2 * core + t, s, z_at][:, :HEAD_DIM] for t in range(2)], 1
+            )
+
+    for sign, hop in hops:
+        early_end(sign, hop)
+    rows_passed(0)
+    keep = [
+        pltpu.make_async_copy(weight_v, weight_out, local.at[5]),
+        pltpu.make_async_copy(rows_v, rows_out, local.at[4]),
+    ]
+    keep[0].start()
+
+    def heads_copy(pair, step):
+        z_to = lax.rem(mine + 4 - step, 4)
+        own = jnp.logical_and(origin == core, z_to == zed)
+        tokens = pl.ds(pl.multiple_of(z_to * share, share), share)
+        on_b = lax.div(pair, 4)
+        row = on_b + (1 - on_b) * 2 * parity
+        target = heads_out.at[row, apart(rolled(lax.rem(pair, 4), zed), z_to), core]
+        return own, heads_v.at[pair, tokens], target, (plane, origin, z_to)
+
+    first_heads = slot("h", 0)
+    for number in range(1, 4 * PAIRS):
+        slot("h", number)
+
+    def attend(pair):
+        row, at = lax.div(pair, 4), lax.rem(pair, 4)
+        z_at = rolled(at, zed)
+        bias = jnp.concatenate([biases_v[z_at, core, j : j + 1] for j in range(3)], 1)
+        for quarter in range(4):
+            part = nt(rows_v[row, quarter], weight_v[at]) + bias
+            qkv_v[pair, quarter * share : (quarter + 1) * share] = part.astype(jnp.bfloat16)
+        forward_pair(
+            slots,
+            qkv_v.at[pair],
+            tab_out[at, :, :128],
+            tab_out[at, :, 128:],
+            seg_out[row].astype(jnp.float32),
+            col_v.at[row],
+            heads_v.at[pair],
+            log_v.at[pair],
+        )
+        for step in range(4):
+            own, source, target, there = heads_copy(pair, step)
+            number = first_heads + 4 * pair + step
+            copy = wires.copy(source, target, number, there)
+
+            @pl.when(own)
+            def _here():
+                pltpu.make_async_copy(source, target, recvs.at[number]).start()
+
+            @pl.when(jnp.logical_not(own))
+            def _there():
+                copy.start()
+
+    pl.loop(0, 2)(attend)
+    for sign in sides:
+        take_late(sign, 2)
+    for sign in sides:
+        take_across(sign, 1)
+    pass_rows(1)
+    pl.loop(2, 4)(attend)
+    for sign in sides:
+        take_late(sign, 3)
+    for sign in sides:
+        take_across(sign, 2)
+    for sign in sides:
+        take_far(sign, 1)
+    rows_passed(1)
+    keep[1].start()
+    pl.loop(4, PAIRS)(attend)
+    for sign in sides:
+        take_across(sign, 3)
+    for sign in sides:
+        take_far(sign, 2)
+    keep.append(pltpu.make_async_copy(qkv_v, qkv_out, local.at[6]))
+    keep[-1].start()
+    log_out[...] = log_v[...]
+    for sign in sides:
+        take_far(sign, 3)
+    for at in range(2):
+        if at:
+            for sign, hop in hops:
+                end_across(sign, hop)
+        side = core if at == 0 else 1 - core
+        keep.append(
+            pltpu.make_async_copy(
+                feed_v.at[:, side, :, : 2 * part_rows], feed_out.at[:, side], local.at[7 + at]
+            )
+        )
+        keep[-1].start()
+        for quarter in range(4):
+            keep.append(
+                pltpu.make_async_copy(
+                    feed_v.at[quarter, side, :, 2 * part_rows :],
+                    proj_out.at[:, side, quarter],
+                    local.at[9 + 4 * at + quarter],
+                )
+            )
+            keep[-1].start()
+    for pair in range(PAIRS):
+        for k in range(4):
+            half, c = k // 2, k % 2
+            step = lax.rem(k + 4 - zed, 4)
+            row = 1 if pair >= 4 else 2 * half
+            target = heads_out.at[row, apart((pair % 4 + 2 * half) % 4, zed), c]
+            wires.got(target, first_heads + 4 * pair + step, (plane, c, 2 * core + half))
+        for step in range(4):
+            own, source, target, there = heads_copy(pair, step)
+            copy = wires.copy(source, target, first_heads + 4 * pair + step, there)
+            pl.when(jnp.logical_not(own))(copy.wait_send)
+    for copy in keep:
+        copy.wait()
+    wires.finish()
+    assert len(slot_at) == FRONT_COPIES, len(slot_at)
+
+
+FRONT_COPIES = 159
+
+
+def front(slots, normed, qkv, bias, table, ids, own):
+    bf16, f32 = jnp.bfloat16, jnp.float32
+    _, share, width = normed.shape
+    seq = 4 * share
+    vmem = pl.BlockSpec(memory_space=pltpu.VMEM)
+    shaped = jax.ShapeDtypeStruct
+    return pl.pallas_call(
+        functools.partial(front_kernel, slots),
+        in_specs=[ANYWHERE] * 6,
+        out_specs=[ANYWHERE] * 6 + [vmem] * 5,
+        out_shape=[
+            shaped((2, 4, share, width), bf16),
+            shaped((4, 384, width), bf16),
+            shaped((PAIRS, seq, 384), bf16),
+            shaped((3, 4, 2, share, 128), bf16),
+            shaped((4, 2, 3, 256, width), bf16),
+            shaped((3, 2, 4, 32, width), bf16),
+            shaped((PAIRS, 2, seq), f32),
+            shaped((4, 16, 256), bf16),
+            shaped((2, 1, seq), jnp.int32),
+            shaped((2, 1, seq), jnp.int32),
+            shaped((8, 4, 128), f32),
+        ],
+        scratch_shapes=[
+            pltpu.SemaphoreType.DMA((FRONT_COPIES,)),
+            pltpu.SemaphoreType.DMA((FRONT_COPIES,)),
+            pltpu.SemaphoreType.DMA((17,)),
+            pltpu.VMEM((2, 4, share, width), bf16),
+            pltpu.VMEM((4, 384, width), bf16),
+            pltpu.VMEM((PAIRS, seq, 384), bf16),
+            pltpu.VMEM((PAIRS, seq, 128), bf16),
+            pltpu.VMEM((PAIRS, 2, seq), f32),
+            pltpu.VMEM((4, 3, 8, 128), f32),
+            pltpu.VMEM((4, 2, 4, 16, 128), bf16),
+            pltpu.VMEM(ids.shape, jnp.int32),
+            pltpu.VMEM(ids.shape, jnp.int32),
+            pltpu.VMEM((2, seq, 128), f32),
+            pltpu.VMEM((4, 2, 3, own.shape[0], width), bf16),
+        ],
+        compiler_params=pltpu.CompilerParams(
+            collective_id=0, has_side_effects=True, vmem_limit_bytes=48 << 20
+        ),
+        cost_estimate=pl.CostEstimate(
+            flops=40_000_000_000, bytes_accessed=60 << 20, transcendentals=8_000_000
+        ),
+        name="front",
+    )(normed, qkv, bias, table, ids, own)
+
+
+def backward_pair(
+    slots, qkv, keys_pre, values_pre, seg_row, seg_col, grads_in, logs, dtab, dbias, dk_acc, dv_acc
+):
+    seq = qkv.shape[0]
+    keys, values = qkv[:, 128:256], qkv[:, 256:384]
+    keys_t = jnp.transpose(keys)
+    keys_pre_t = jnp.transpose(keys_pre)
+    pre_row = lax.broadcasted_iota(jnp.int32, (keys_pre.shape[0], QB), 0)
+    zero = jnp.zeros((keys_pre.shape[0], 128), jnp.float32)
+    dtab_k, dtab_v, dq_sum = zero, zero, jnp.zeros((1, 128), jnp.float32)
+    for block in reversed(range(seq // QB)):
+        extent = (block + 1) * QB
+        here = slice(block * QB, extent)
+        visible = visible_to(seg_col, seg_row, block)
+        queries = qkv[here, :128] * 0.125
+        grads = grads_in[here, :]
+        weights, dscores, weights_pre, dscores_pre, query_halves, grad_halves, dq_parts = (
+            [], [], [], [], [], [], [],
+        )
+        for head in range(2):
+            rows = slice(head * HEAD_DIM, (head + 1) * HEAD_DIM)
+            query, grad = half_mask(queries, head), half_mask(grads, head)
+            log_total = logs[head : head + 1, here]
+            s_tok = jnp.where(visible, nt(keys[:extent], query), MASKED)
+            s_pre = jnp.where(pre_row < slots, nt(keys_pre, query), MASKED)
+            w_tok, w_pre = jnp.exp(s_tok - log_total), jnp.exp(s_pre - log_total)
+            dp_tok, dp_pre = nt(values[:extent], grad), nt(values_pre, grad)
+            delta = jnp.sum(w_tok * dp_tok, 0, keepdims=True) + jnp.sum(
+                w_pre * dp_pre, 0, keepdims=True
+            )
+            ds_tok = (w_tok * (dp_tok - delta)).astype(jnp.bfloat16)
+            ds_pre = (w_pre * (dp_pre - delta)).astype(jnp.bfloat16)
+            dq_parts.append(nn(keys_t[rows, :extent], ds_tok) + nn(keys_pre_t[rows], ds_pre))
+            weights.append(w_tok.astype(jnp.bfloat16))
+            weights_pre.append(w_pre.astype(jnp.bfloat16))
+            dscores.append(ds_tok)
+            dscores_pre.append(ds_pre)
+            query_halves.append(query)
+            grad_halves.append(grad)
+        query_both = jnp.concatenate(query_halves, 0)
+        grad_both = jnp.concatenate(grad_halves, 0)
+        dv = nn(jnp.concatenate(weights, 1), grad_both)
+        dk = nn(jnp.concatenate(dscores, 1), query_both)
+        if block == seq // QB - 1:
+            dv_acc[...] = dv
+            dk_acc[...] = dk
+        else:
+            dv_acc[:extent] += dv
+            dk_acc[:extent] += dk
+        dtab_v = dtab_v + nn(jnp.concatenate(weights_pre, 1), grad_both)
+        dtab_k = dtab_k + nn(jnp.concatenate(dscores_pre, 1), query_both)
+        dq = jnp.transpose(jnp.concatenate(dq_parts, 0)) * 0.125
+        dq_sum = dq_sum + jnp.sum(dq, 0, keepdims=True)
+        qkv[here, :128] = dq.astype(jnp.bfloat16)
+    dk, dv = dk_acc[...], dv_acc[...]
+    qkv[:, 128:256] = dk.astype(jnp.bfloat16)
+    qkv[:, 256:384] = dv.astype(jnp.bfloat16)
+    dbias[...] = jnp.concatenate(
+        [dq_sum, jnp.sum(dk, 0, keepdims=True), jnp.sum(dv, 0, keepdims=True)], 1
+    )
+    dtab[:, :128] = dtab_k
+    dtab[:, 128:] = dtab_v
+
+
+def add_up(rows, target, *sources):
+    chunk = 96 if rows % 96 == 0 else 64
+
+    @pl.loop(0, rows // chunk)
+    def _add(at):
+        span = pl.ds(pl.multiple_of(at * chunk, 32), chunk)
+        if len(sources) == 2:
+            target[span] = sources[0][span] + sources[1][span]
+            return
+        value = sources[0][span].astype(jnp.float32)
+        for source in sources[1:]:
+            value = value + source[span].astype(jnp.float32)
+        target[span] = value.astype(jnp.bfloat16)
+
+
+def back_kernel(
+    slots,
+    heads_ref, feed_ref, proj_ref, qkv_ref, rows_ref, weight_ref,
+    log_ref, tab_ref, seg_ref, live_ref, small_ref, tokens_ref, rout_ref,
+    full_out, back_out, first_out, second_out,
+    sends, recvs, local,
+    dh_v, sib_v, own_v, plane_v, sum_v, z_v, gq_v, plane_q, sum_q, z_q, done_v,
+    qkv_v, weight_v, df_v, dfs_v, col_v, dk_acc, dv_acc,
+    dtab_v, dbias_v, back_v, first_v, first_in, second_v, second_in,
+):
+    plane, core, zed = position()
+    parity = lax.rem(zed, 2)
+    mine = 2 * parity + core
+    origin = lax.div(zed, 2)
+    sibling = (plane, 1 - core, zed)
+    share = heads_ref.shape[3]
+    seq = 4 * share
+    feed_rows, proj_rows = feed_ref.shape[3], proj_ref.shape[3]
+    both = feed_rows + proj_rows
+    q_rows = gq_v.shape[2]
+    around = [(plane_at(plane, offset), core, zed) for offset in range(4)]
+    ahead = [lax.rem(zed + step, 4) for step in range(4)]
+    greet(column_partners() + plane_partners())
+    wires = Wires(sends, recvs)
+    slot_at = {}
+
+    def slot(*name):
+        return slot_at.setdefault(name, len(slot_at))
+
+    tokens = pl.ds(pl.multiple_of(zed * share, share), share)
+    first_heads = slot("h", 0)
+    for number in range(1, 4 * PAIRS):
+        slot("h", number)
+    for pair in range(PAIRS):
+        for step in range(4):
+            k = ahead[step]
+            half, c = lax.div(k, 2), lax.rem(k, 2)
+            z_to = 2 * core + half
+            own = jnp.logical_and(c == core, z_to == zed)
+            row = 1 if pair >= 4 else 2 * half
+            wires.put_unless(
+                own,
+                heads_ref.at[row, lax.rem(pair % 4 + 2 * half + 4 - zed, 4), c],
+                dh_v.at[pair, tokens],
+                first_heads + 4 * pair + step,
+                (plane, c, z_to),
+            )
+    turns = [lax.rem(zed + 1 + turn, 4) for turn in range(4)]
+    own_copies = []
+    for turn in range(4):
+        z_at = (turn + 1) % 4
+        wires.put(
+            feed_ref.at[:, 1 - core, z_at], sib_v.at[turn, :, :feed_rows], slot("s", turn), sibling
+        )
+        wires.put(
+            proj_ref.at[z_at, 1 - core], sib_v.at[turn, :, feed_rows:], slot("sp", turn), sibling
+        )
+        own_copies.append(
+            [
+                pltpu.make_async_copy(
+                    feed_ref.at[:, core, z_at],
+                    own_v.at[turn % 2, :, :feed_rows],
+                    local.at[2 * (turn % 2)],
+                ),
+                pltpu.make_async_copy(
+                    proj_ref.at[z_at, core],
+                    own_v.at[turn % 2, :, feed_rows:],
+                    local.at[2 * (turn % 2) + 1],
+                ),
+            ]
+        )
+    later = [
+        pltpu.make_async_copy(qkv_ref, qkv_v, local.at[4]),
+        pltpu.make_async_copy(weight_ref, weight_v, local.at[5]),
+    ]
+    for copy in own_copies[0] + own_copies[1] + later:
+        copy.start()
+    for row in range(2):
+        line = jnp.where(live_ref[row] > 0, seg_ref[row], -1).astype(jnp.float32)
+        col_v[row] = jnp.transpose(jnp.broadcast_to(line, (128, seq)))
+
+    def chip_sum(turn):
+        for copy in own_copies[turn]:
+            copy.wait()
+        wires.got(sib_v.at[turn, :, :feed_rows], slot("s", turn), sibling)
+        wires.got(sib_v.at[turn, :, feed_rows:], slot("sp", turn), sibling)
+        for at in range(4):
+            add_up(both, sib_v.at[turn, at], sib_v.at[turn, at], own_v.at[turn % 2, at])
+        if turn < 2:
+            for copy in own_copies[turn + 2]:
+                copy.start()
+        first, _ = axes(turn)
+        for kind, offset in enumerate((3, first)):
+            wires.put(
+                sib_v.at[turn, plane_at(plane, offset)],
+                plane_v.at[kind, turn],
+                slot("p", turn, kind),
+                around[first],
+            )
+
+    def axes(turn):
+        return (1, 2) if turn % 2 else (2, 1)
+
+    def merge(turn):
+        first, other = axes(turn)
+        wires.got(plane_v.at[0, turn], slot("p", turn, 0), around[first])
+        target = sib_v.at[turn, plane_at(plane, other)]
+        add_up(both, target, target, plane_v.at[0, turn])
+        wires.put(target, plane_v.at[2, turn], slot("p", turn, 2), around[other])
+
+    chip_sum(0)
+    chip_sum(1)
+    for copy in later:
+        copy.wait()
+
+    def heads_here(pairs):
+        for pair in pairs:
+            for step in range(4):
+                z_from = lax.rem(mine + 4 - step, 4)
+                there = pl.ds(pl.multiple_of(z_from * share, share), share)
+                wires.got(dh_v.at[pair, there], first_heads + 4 * pair + step, sibling)
+
+    def attend(pair):
+        row, at = lax.div(pair, 4), lax.rem(pair, 4)
+        backward_pair(
+            slots,
+            qkv_v.at[pair],
+            tab_ref[at, :, :128],
+            tab_ref[at, :, 128:],
+            seg_ref[row].astype(jnp.float32),
+            col_v.at[row],
+            dh_v.at[pair],
+            log_ref.at[pair],
+            dtab_v.at[pair],
+            dbias_v.at[pair],
+            dk_acc,
+            dv_acc,
+        )
+
+    def plane_sum(turn):
+        for kind, offset in zip((1, 2), axes(turn)):
+            wires.got(plane_v.at[kind, turn], slot("p", turn, kind), around[offset])
+        add_up(
+            both, sum_v.at[turn], sib_v.at[turn, plane], *[plane_v.at[j, turn] for j in (1, 2)]
+        )
+        if turn < 3:
+            wires.put(
+                sum_v.at[turn], z_v.at[turn], slot("z", turn), (plane, core, turns[turn])
+            )
+
+    low = lax.rem(zed, 2)
+    partners = [
+        sibling, around[1], around[2],
+        (plane, core, zed + 1 - 2 * low), (plane, core, ahead[2]),
+    ]
+
+    def small_send(name, values, arrived, step):
+        wires.put(values.at[step], arrived.at[step], slot(name, step), partners[step])
+
+    def small_take(name, values, arrived, step):
+        wires.got(arrived.at[step], slot(name, step), partners[step])
+        values[step + 1] = values[step] + arrived[step]
+        if step < 4:
+            small_send(name, values, arrived, step + 1)
+
+    def first_sums():
+        first_v[0] = jnp.zeros(first_v.shape[1:], jnp.float32)
+        first_v[0, :64] = small_ref[...]
+        for at in range(4):
+            entry = core * 4 + lax.rem(at + 2 * parity, 4)
+            table, bias = dtab_v[at], dbias_v[at]
+            if at < 2:
+                table, bias = table + dtab_v[4 + at], bias + dbias_v[4 + at]
+            base = pl.multiple_of(64 + 32 * entry, 8)
+            first_v[0, pl.ds(base, 16)] = table[:, :128]
+            first_v[0, pl.ds(base + 16, 16)] = table[:, 128:]
+            base = pl.multiple_of(320 + 8 * entry, 8)
+            first_v[0, pl.ds(base, 8)] = jnp.concatenate(
+                [bias[:, :128], bias[:, 128:256], bias[:, 256:], jnp.zeros((5, 128), jnp.float32)], 0
+            )
+        small_send("a", first_v, first_in, 0)
+
+    def tanh_part():
+        entry = lax.div(plane, 2) * 4 + zed
+        base = pl.multiple_of(64 + 32 * entry + 16 * core, 8)
+        table = first_v[5, pl.ds(base, 16)]
+        table = jnp.where(lax.rem(plane, 2) == 0, table[:, :HEAD_DIM], table[:, HEAD_DIM:])
+        part = lax.dot_general(
+            table,
+            rout_ref[...].astype(jnp.float32),
+            (((1,), (1,)), ((), ())),
+            preferred_element_type=jnp.float32,
+            precision=HIGHEST,
+        )
+        for j in range(4):
+            second_v[0, 16 * j : 16 * j + 16] = part[:, 128 * j : 128 * j + 128]
+
+    def norm_sums():
+        span_rows = 64
+
+        def body(at, sums):
+            row, part = lax.div(at, share // span_rows), lax.rem(at, share // span_rows)
+            span = pl.ds(pl.multiple_of(part * span_rows, span_rows), span_rows)
+            grad = back_v[row, span].astype(jnp.float32)
+            extra = back_v[3, span].astype(jnp.float32)
+            grad = grad + jnp.where(row == 1, extra, 0.0)
+            hat, _ = normalize(tokens_ref[row, span].astype(jnp.float32))
+            return (
+                sums[0] + jnp.sum(grad * hat, 0, keepdims=True),
+                sums[1] + jnp.sum(grad, 0, keepdims=True),
+            )
+
+        zero = jnp.zeros((1, back_v.shape[2]), jnp.float32)
+        sums = lax.fori_loop(0, 3 * (share // span_rows), body, (zero, zero))
+        for kind in range(2):
+            for j in range(8):
+                at = 64 + 8 * kind + j
+                second_v[0, at : at + 1] = sums[kind][:, 128 * j : 128 * j + 128]
+        small_send("b", second_v, second_in, 0)
+
+    first_row = slot("r", 0)
+    for number in range(1, 4):
+        slot("r", number)
+
+    def row_grads(kind):
+        for quarter in range(4):
+            span = slice(quarter * share, (quarter + 1) * share)
+            parts = [
+                nn(qkv_v[4 * kind + at, span], weight_v[at]) for at in range(2 if kind else 4)
+            ]
+            total = parts[0] + parts[1]
+            for part in parts[2:]:
+                total = total + part
+            df_v[kind, quarter] = total.astype(jnp.bfloat16)
+            wires.put_if(
+                core != kind, df_v.at[kind, quarter], dfs_v.at[quarter], slot("df", quarter, kind),
+                sibling,
+            )
+
+    def send_rows(kind):
+        here = core == kind
+        for quarter in range(4):
+            wires.got_if(here, dfs_v.at[quarter], slot("df", quarter, kind), sibling)
+
+            @pl.when(here)
+            def _sum():
+                add_up(share, dfs_v.at[quarter], dfs_v.at[quarter], df_v.at[kind, quarter])
+
+        for step in range(4):
+            z_to = lax.rem(2 * parity + kind + 4 - step, 4)
+            own = jnp.logical_and(origin == core, z_to == zed)
+            source, target = dfs_v.at[z_to], back_v.at[2 * parity + kind]
+
+            @pl.when(jnp.logical_and(here, own))
+            def _here():
+                pltpu.make_async_copy(source, target, recvs.at[first_row + step]).start()
+
+            wires.put_if(
+                jnp.logical_and(here, jnp.logical_not(own)),
+                source,
+                target,
+                first_row + step,
+                (plane, origin, z_to),
+            )
+
+    heads_here((0, 1))
+    pl.loop(0, 2)(attend)
+    chip_sum(2)
+    merge(0)
+    heads_here((2, 3))
+    pl.loop(2, 4)(attend)
+    chip_sum(3)
+    merge(1)
+    rows_v = own_v
+    row_copy = pltpu.make_async_copy(rows_ref, rows_v.at[:, :, :share], local.at[0])
+    row_copy.start()
+    plane_sum(0)
+    row_grads(0)
+    merge(2)
+    heads_here((4, 5))
+    pl.loop(4, PAIRS)(attend)
+    merge(3)
+    plane_sum(1)
+    first_sums()
+    send_rows(0)
+    row_grads(1)
+    plane_sum(2)
+    small_take("a", first_v, first_in, 0)
+    row_copy.wait()
+    rows_a = jnp.concatenate([rows_v[0, j, :share] for j in range(4)], 0)
+    for at in range(4):
+        grad = outer_sum(qkv_v[at], rows_a)
+        if at < 2:
+            grad = grad + outer_sum(
+                qkv_v[4 + at], jnp.concatenate([rows_v[1, j, :share] for j in range(4)], 0)
+            )
+        grad = grad.astype(jnp.bfloat16)
+        for j in range(4):
+            gq_v[at, j] = grad[j * q_rows : (j + 1) * q_rows]
+        if at % 2:
+            sub = at // 2
+            slots_here = slice(at - 1, at + 1)
+            first, _ = axes(sub)
+            for kind, offset in enumerate((3, first)):
+                wires.put(
+                    gq_v.at[slots_here, plane_at(plane, offset)],
+                    plane_q.at[kind, slots_here],
+                    slot("pq", sub, kind),
+                    around[first],
+                )
+    small_take("a", first_v, first_in, 1)
+    send_rows(1)
+    plane_sum(3)
+    small_take("a", first_v, first_in, 2)
+    for sub in range(2):
+        first, other = axes(sub)
+        slots_here = slice(2 * sub, 2 * sub + 2)
+        wires.got(plane_q.at[0, slots_here], slot("pq", sub, 0), around[first])
+        at_other = plane_at(plane, other)
+        for at in (2 * sub, 2 * sub + 1):
+            target = gq_v.at[at, at_other]
+            add_up(q_rows, target, target, plane_q.at[0, at])
+        wires.put(
+            gq_v.at[slots_here, at_other], plane_q.at[2, slots_here], slot("pq", sub, 2), around[other]
+        )
+    small_take("a", first_v, first_in, 3)
+
+    def spread(name, span_of):
+        copy = pltpu.make_async_copy(
+            done_v.at[span_of(2)],
+            full_out.at[plane, core, span_of(2)],
+            local.at[6 if name == "f" else 7],
+        )
+        copy.start()
+        for half in range(2):
+            for offset in (1, 2) if half == 0 else (2, 1):
+                wires.put(
+                    done_v.at[span_of(half)],
+                    full_out.at[plane, core, span_of(half)],
+                    slot(name, half, offset),
+                    around[offset],
+                )
+        wires.put(
+            done_v.at[span_of(2)], full_out.at[plane, core, span_of(2)], slot(name, 2, 0), sibling
+        )
+        return copy
+
+    def spread_on(name, span_of):
+        for half in range(2):
+            came, goes = (1, 2) if half == 0 else (2, 1)
+            piece = full_out.at[plane_at(plane, came), core, span_of(half)]
+            wires.got(piece, slot(name, half, came), around[came])
+            wires.put(piece, piece, slot(name, half, 3), around[goes])
+        for half in range(2):
+            came = 2 if half == 0 else 1
+            piece = full_out.at[plane_at(plane, came), core, span_of(half)]
+            wires.got(piece, slot(name, half, came), around[came])
+        for offset in (1, 2):
+            piece = full_out.at[plane_at(plane, offset), core, span_of(2)]
+            wires.put(piece, piece, slot(name, 2, offset), sibling)
+
+    def spread_far(name, span_of):
+        for half in range(2):
+            piece = full_out.at[plane_at(plane, 3), core, span_of(half)]
+            wires.got(piece, slot(name, half, 3), around[2 if half == 0 else 1])
+        piece = full_out.at[plane_at(plane, 3), core, span_of(2)]
+        wires.put(piece, piece, slot(name, 2, 3), sibling)
+
+    def spread_end(name, span_of):
+        for offset in range(4):
+            wires.got(
+                full_out.at[plane_at(plane, offset), 1 - core, span_of(2)],
+                slot(name, 2, offset),
+                sibling,
+            )
+
+    def feed_span(half):
+        return (pl.ds(0, both // 2), pl.ds(both // 2, both // 2), pl.ds(0, both))[half]
+
+    def q_span(half):
+        return (
+            pl.ds(both, q_rows // 2), pl.ds(both + q_rows // 2, q_rows // 2), pl.ds(both, q_rows)
+        )[half]
+
+    for turn in range(3):
+        wires.got(z_v.at[turn], slot("z", turn), (plane, core, lax.rem(zed + 3 - turn, 4)))
+    add_up(both, done_v.at[feed_span(2)], sum_v.at[3], *[z_v.at[j] for j in range(3)])
+    last = [spread("f", feed_span)]
+    small_take("a", first_v, first_in, 4)
+    tanh_part()
+    for sub in range(2):
+        slots_here = slice(2 * sub, 2 * sub + 2)
+        for kind, offset in zip((1, 2), axes(sub)):
+            wires.got(plane_q.at[kind, slots_here], slot("pq", sub, kind), around[offset])
+        for at in (2 * sub, 2 * sub + 1):
+            add_up(q_rows, sum_q.at[at], gq_v.at[at, plane], *[plane_q.at[j, at] for j in (1, 2)])
+    for turn in range(3):
+        wires.put(
+            sum_q.at[lax.rem(turns[turn] + 2 * parity, 4)],
+            z_q.at[turn],
+            slot("zq", turn),
+            (plane, core, turns[turn]),
+        )
+    spread_on("f", feed_span)
+    for k in range(4):
+        wires.got(
+            back_v.at[k],
+            first_row + lax.rem(k + 4 - zed, 4),
+            (plane, k % 2, 2 * core + k // 2),
+        )
+    last.append(pltpu.make_async_copy(back_v, back_out, local.at[8]))
+    last[-1].start()
+    norm_sums()
+    for turn in range(3):
+        wires.got(z_q.at[turn], slot("zq", turn), (plane, core, lax.rem(zed + 3 - turn, 4)))
+    add_up(
+        q_rows,
+        done_v.at[q_span(2)],
+        sum_q.at[lax.rem(zed + 2 * parity, 4)],
+        *[z_q.at[j] for j in range(3)],
+    )
+    last.append(spread("q", q_span))
+    small_take("b", second_v, second_in, 0)
+    spread_far("f", feed_span)
+    small_take("b", second_v, second_in, 1)
+    spread_on("q", q_span)
+    small_take("b", second_v, second_in, 2)
+    spread_far("q", q_span)
+    small_take("b", second_v, second_in, 3)
+    small_take("b", second_v, second_in, 4)
+    first_out[...] = first_v[5]
+    second_out[...] = second_v[5]
+    spread_end("f", feed_span)
+    spread_end("q", q_span)
+    for copy in last:
+        copy.wait()
+    wires.finish()
+    assert len(slot_at) == BACK_COPIES, len(slot_at)
+
+
+BACK_COPIES = 98
+
+
+def back(
+    slots, d_heads, grad_feed, grad_out, qkv, rows, weights, logs, tab, seg, live, small, tokens, rout
+):
+    bf16, f32 = jnp.bfloat16, jnp.float32
+    share, width = rows.shape[2:]
+    seq = 4 * share
+    vmem = pl.BlockSpec(memory_space=pltpu.VMEM)
+    shaped, held = jax.ShapeDtypeStruct, pltpu.VMEM
+    both, q_rows = grad_feed.shape[3] + grad_out.shape[3], 96
+    return pl.pallas_call(
+        functools.partial(back_kernel, slots),
+        in_specs=[ANYWHERE] * 6 + [vmem] * 7,
+        out_specs=[ANYWHERE] * 2 + [vmem] * 2,
+        out_shape=[
+            shaped((4, 2, both + q_rows, width), bf16),
+            shaped((4, share, width), bf16),
+            shaped((384, 128), f32),
+            shaped((80, 128), f32),
+        ],
+        scratch_shapes=[
+            pltpu.SemaphoreType.DMA((BACK_COPIES,)),
+            pltpu.SemaphoreType.DMA((BACK_COPIES,)),
+            pltpu.SemaphoreType.DMA((9,)),
+            held((PAIRS, seq, 128), bf16),
+            held((4, 4, both, width), bf16),
+            held((2, 4, both, width), bf16),
+            held((3, 4, both, width), bf16),
+            held((4, both, width), bf16),
+            held((3, both, width), bf16),
+            held((4, 4, q_rows, width), bf16),
+            held((3, 4, q_rows, width), bf16),
+            held((4, q_rows, width), bf16),
+            held((3, q_rows, width), bf16),
+            held((both + q_rows, width), bf16),
+            held((PAIRS, seq, 384), bf16),
+            held((4, 384, width), bf16),
+            held((2, 4, share, width), bf16),
+            held((4, share, width), bf16),
+            held((2, seq, 128), f32),
+            held((seq, 128), f32),
+            held((seq, 128), f32),
+            held((PAIRS, 16, 256), f32),
+            held((PAIRS, 1, 384), f32),
+            held((4, share, width), bf16),
+            held((6, 384, 128), f32),
+            held((5, 384, 128), f32),
+            held((6, 80, 128), f32),
+            held((5, 80, 128), f32),
+        ],
+        compiler_params=pltpu.CompilerParams(
+            collective_id=2, has_side_effects=True, vmem_limit_bytes=62 << 20
+        ),
+        cost_estimate=pl.CostEstimate(
+            flops=80_000_000_000, bytes_accessed=60 << 20, transcendentals=8_000_000
+        ),
+        name="back",
+    )(
+        d_heads, grad_feed, grad_out, qkv, rows, weights, logs, tab, seg, live, small, tokens, rout
+    )
+
+
+def write_feed_kernel(piece_ref, up_ref, down_ref):
+    for c in range(2):
+        span = slice(128 * c, 128 * c + 128)
+        up_ref[:, span] = jnp.transpose(piece_ref[0, c, :128].astype(jnp.float32))
+        down_ref[span] = piece_ref[0, c, 128:].astype(jnp.float32)
+
+
+def write_rest_kernel(piece_ref, grad_ref, out_ref):
+    for at in range(4):
+        out_ref[32 * at : 32 * at + 32] = piece_ref[at, 0, :32].astype(jnp.float32)
+    turned = [jnp.transpose(piece_ref[at, 0, 32:].astype(jnp.float32)) for at in range(4)]
+    turned = jnp.concatenate(turned, 1)
+    order = [(kind, head) for head in range(2) for kind in range(3)]
+    grad_ref[...] = jnp.concatenate(
+        [turned[:, 128 * kind + 64 * head : 128 * kind + 64 * head + 64] for kind, head in order], 1
+    )
+
+
+def write_grads(full):
+    f32 = jnp.float32
+    width = full.shape[3]
+    up, down = pl.pallas_call(
+        write_feed_kernel,
+        grid=(4,),
+        in_specs=[pl.BlockSpec((1, 2, 256, width), lambda p: (p, 0, 0, 0))],
+        out_specs=[
+            pl.BlockSpec((width, 256), lambda p: (0, p)),
+            pl.BlockSpec((256, width), lambda p: (p, 0)),
+        ],
+        out_shape=[
+            jax.ShapeDtypeStruct((width, 1024), f32),
+            jax.ShapeDtypeStruct((1024, width), f32),
+        ],
+        name="write_feed",
+    )(full)
+    qkv, out = pl.pallas_call(
+        write_rest_kernel,
+        grid=(2,),
+        in_specs=[pl.BlockSpec((4, 1, 128, width), lambda c: (0, c, 2, 0))],
+        out_specs=[
+            pl.BlockSpec((width, 384), lambda c: (0, c)),
+            pl.BlockSpec((128, width), lambda c: (c, 0)),
+        ],
+        out_shape=[
+            jax.ShapeDtypeStruct((width, 768), f32),
+            jax.ShapeDtypeStruct((256, width), f32),
+        ],
+        compiler_params=pltpu.CompilerParams(vmem_limit_bytes=40 << 20),
+        name="write_rest",
+    )(full)
+    return up, down, out, qkv
+
+
+def per_device_fast(
+    tokens,
+    segment_ids,
+    row_lengths,
+    ln1_gain,
+    ln1_bias,
+    qkv_weight,
+    qkv_bias,
+    out_weight,
+    out_bias,
+    ln2_gain,
+    ln2_bias,
+    up_weight,
+    up_bias,
+    down_weight,
+    down_bias,
+    prefix_embed,
+    reparam_in,
+    reparam_in_bias,
+    reparam_out,
+    reparam_out_bias,
+    cotangent,
+):
+    bf16, f32 = jnp.bfloat16, jnp.float32
+    plane, core, zed = lax.axis_index("pl"), lax.axis_index("core"), lax.axis_index("mp")
+    micro, share, width = tokens.shape
+    seq = segment_ids.shape[1]
+    slots = prefix_embed.shape[0]
+
+    def pick(stack, index):
+        return lax.dynamic_index_in_dim(stack, index, 0, keepdims=False)
+
+    pre_act = nn(prefix_embed, reparam_in) + reparam_in_bias
+    tanh_hidden = jnp.tanh(pre_act)
+    tanh_low = tanh_hidden.astype(bf16)
+    table_part = (nn(tanh_low, reparam_out) + reparam_out_bias).astype(bf16)
+    table_part = jnp.pad(table_part, ((0, 16 - slots), (0, 128 - HEAD_DIM)))
+    packed_ids = jnp.concatenate(
+        [segment_ids, jnp.broadcast_to(row_lengths[:, :1], (micro, 128))], 1
+    )
+    packed_ids = jnp.pad(packed_ids, ((0, 8 - micro), (0, 0)))[:, None]
+    packed_bias = jnp.concatenate(
+        [
+            jnp.pad(
+                qkv_bias.reshape(2, 2, 3, HEAD_DIM).transpose(0, 2, 1, 3).reshape(2, 3, 128),
+                ((0, 0), (0, 5), (0, 0)),
+            ),
+            up_bias.reshape(1, 8, 128),
+        ]
+    )
+    x_share = tokens.astype(f32)
+    hat_first, inverse_first = normalize(x_share)
+    normed_first = (hat_first * ln1_gain + ln1_bias).astype(bf16)
+    qkv_half = lax.dynamic_index_in_dim(
+        qkv_weight.reshape(width, 2, 2, 3, HEAD_DIM), core, 1, keepdims=False
+    )
+    qkv_half = qkv_half.transpose(2, 1, 3, 0).reshape(384, width)
+    down_own = down_weight.reshape(8, 128, width)
+    (
+        normed_home, qkv_full, qkv, heads_rows, feed_full, out_full, logs, tab, seg, live, biases
+    ) = front(
+        slots,
+        normed_first,
+        qkv_half,
+        packed_bias,
+        table_part,
+        packed_ids,
+        jnp.concatenate(
+            [
+                lax.dynamic_slice_in_dim(up_weight, (2 * plane + core) * 128, 128, 1).T,
+                pick(down_own, 2 * plane + core),
+                lax.dynamic_slice_in_dim(out_weight, core * 128 + plane * 32, 32, 0),
+            ]
+        ),
+    )
+    up_bias_all = biases.reshape(8, 1, 512)
+    block_out, d_resid, d_heads, grad_out, sums, grad_feed, grad_up_bias = feed_forward(
+        heads_rows,
+        tokens.reshape(3 * share, width),
+        cotangent.reshape(3 * share, width),
+        out_weight,
+        out_full.reshape(3 * 256, width),
+        jnp.stack([out_bias, ln2_gain, ln2_bias, down_bias]),
+        up_weight,
+        down_own,
+        feed_full.reshape(8, 3, 256, width),
+        up_bias_all,
+    )
+    block_out = block_out.reshape(tokens.shape)
+    grad_feed = grad_feed.reshape(4, 2, 4, 256, width)
+    grad_out = grad_out.reshape(4, 2, 4, 32, width)
+    small = jnp.concatenate(
+        [
+            jnp.roll(grad_up_bias.reshape(8, 4, 128), zed, 1).reshape(32, 128),
+            sums.reshape(32, 128),
+        ]
+    )
+    full, came, first, second = back(
+        slots,
+        d_heads,
+        grad_feed,
+        grad_out,
+        qkv,
+        normed_home,
+        qkv_full,
+        logs,
+        tab,
+        seg,
+        live,
+        small,
+        tokens,
+        reparam_out,
+    )
+    came = came.astype(f32)
+    d_first = jnp.stack([came[0], came[1] + came[3], came[2]])
+    input_grad = d_resid.reshape(tokens.shape) + norm_back(
+        d_first, hat_first, inverse_first, ln1_gain
+    )
+    grad_up, grad_down, grad_out, grad_qkv = write_grads(full)
+    grad_up_bias = pick(first[:32].reshape(8, 4, 128).transpose(1, 0, 2).reshape(4, 1024), zed)
+    ln2_gain_grad, ln2_bias_grad, out_bias_grad, down_bias_grad = first[32:64].reshape(4, width)
+    table_own = first[64:320].reshape(2, 4, 2, 16, 2, HEAD_DIM)
+    table_own = table_own[plane // 2, zed, core, :slots, plane % 2]
+    grad_qkv_bias = pick(
+        first[320:].reshape(2, 4, 8, 2, HEAD_DIM).transpose(1, 0, 3, 2, 4)[..., :3, :], zed
+    ).reshape(768)
+    grad_rout = jnp.dot(tanh_low.astype(f32).T, table_own, precision=HIGHEST)
+    grad_rout_bias = jnp.sum(table_own, 0)
+    tanh_sum = second[:64].reshape(4, 16, 128).transpose(1, 0, 2).reshape(16, 512)[:slots]
+    ln1_gain_grad, ln1_bias_grad = second[64:].reshape(2, width)
+    d_pre = tanh_sum * (1.0 - tanh_hidden * tanh_hidden)
+    grad_rin = jnp.dot(prefix_embed.astype(f32).T, d_pre, precision=HIGHEST)
+    grad_rin_bias = jnp.sum(d_pre, 0)
+    grad_embed = jnp.dot(d_pre, reparam_in.astype(f32).T, precision=HIGHEST)
+    return (
+        block_out,
+        input_grad,
+        ln1_gain_grad,
+        ln1_bias_grad,
+        grad_qkv,
+        grad_qkv_bias,
+        grad_out,
+        out_bias_grad,
+        ln2_gain_grad,
+        ln2_bias_grad,
+        grad_up,
+        grad_up_bias,
+        grad_down,
+        down_bias_grad,
+        grad_embed,
+        grad_rin,
+        grad_rin_bias,
+        grad_rout,
+        grad_rout_bias,
+    )
+
+
+def specs(dp, mp):
+    rows = P(None, dp + mp, None)
+    ins = (
+        rows, P(None, dp), P(None, dp), P(), P(), P(None, mp), P(mp), P(mp, None), P(), P(), P(),
+        P(None, mp), P(mp), P(mp, None), P(), P(), P(), P(), P(None, mp + dp), P(mp + dp), rows,
+    )
+    outs = (
+        rows, rows, P(), P(), P(None, mp), P(mp), P(mp, None), P(), P(), P(), P(None, mp), P(mp),
+        P(mp, None), P(), P(), P(), P(), P(None, mp + dp), P(mp + dp),
+    )
+    return ins, outs
+
+
 def solution(mesh):
-    placed = (
-        P(None, ("dp", "mp"), None),
-        P(None, "dp"),
-        P(None, "dp"),
-        P(),
-        P(),
-        P(None, "mp"),
-        P("mp"),
-        P("mp", None),
-        P(),
-        P(),
-        P(),
-        P(None, "mp"),
-        P("mp"),
-        P("mp", None),
-        P(),
-        P(),
-        P(),
-        P(),
-        P(None, ("mp", "dp")),
-        P(("mp", "dp")),
-        P(None, ("dp", "mp"), None),
-    )
-    return jax.shard_map(
-        per_device,
-        mesh=mesh,
-        in_specs=placed,
-        out_specs=(
-            P(None, ("dp", "mp"), None),
-            P(None, ("dp", "mp"), None),
-            P(),
-            P(),
-            P(None, "mp"),
-            P("mp"),
-            P("mp", None),
-            P(),
-            P(),
-            P(),
-            P(None, "mp"),
-            P("mp"),
-            P("mp", None),
-            P(),
-            P(),
-            P(),
-            P(),
-            P(None, ("mp", "dp")),
-            P(("mp", "dp")),
-        ),
-        check_vma=False,
-    )
+    if mesh.shape["dp"] == 8 and mesh.shape["mp"] == 4:
+        body = per_device_fast
+        grid = jax.sharding.Mesh(mesh.devices.reshape(4, 2, 4), ALL)
+        ins, outs = specs(("pl", "core"), ("mp",))
+    else:
+        body = per_device
+        grid = mesh
+        ins, outs = specs(("dp",), ("mp",))
+    return jax.shard_map(body, mesh=grid, in_specs=ins, out_specs=outs, check_vma=False)

time: 1700 us -> 486 us (0.29)
  waiting for transfers between devices: 1020 us -> 0 us
  Pallas kernels: 0 us -> 439 us
  matrix products: 305 us -> 3.88 us
  other arithmetic: 202 us -> 11.7 us
  blocking collectives: 114 us -> 0 us
    pallas_call x0 -> x5, Pallas kernels: none -> 439 us  [the longest x1 205 us: back(): pl.pallas_call(functools.partial(back_kernel, slots), in_specs=[ANYWHERE]...]
    all_gather x12 -> x0, waiting for transfers between devices: 425 us -> none  [the longest x3 128 us: micro_step(): lax.all_gather((hat_second * ln2_gain + ln2_bias).astype(jnp.bfloat16), '...]
    reduce_scatter x12 -> x0, waiting for transfers between devices: 349 us -> none  [the longest x3 128 us: micro_step(): lax.psum_scatter(product_transposed(d_up, up_weight).astype(jnp.bfloat16)...]
    dot_general x78 -> x5, matrix products: 305 us -> 3.88 us  [the longest x1 1.56 us: per_device_fast(): grad_embed = jnp.dot(d_pre, reparam_in.astype(f32).T, precision=HIGHEST)]
    psum x3 -> x0, waiting for transfers between devices: 212 us -> none  [micro_step(): lax.psum(grad_qkv.astype(jnp.bfloat16), 'dp').astype(jnp.float32)]
    psum x4 -> x0, blocking collectives: 85.4 us -> none  [the longest x3 44.4 us: micro_step(): lax.psum(grad_qkv_bias.astype(jnp.bfloat16), 'dp').astype(jnp.float32)]
    add x36 -> x2, other arithmetic: 65.8 us -> 2.45 us  [the longest x1 2.27 us: per_device_fast(): d_resid.reshape(tokens.shape)]
    convert_element_type x15 -> x2, other arithmetic: 53.5 us -> 3.97 us  [the longest x1 2.19 us: per_device_fast(): came = came.astype(f32)]
  transfers between devices with their start and end apart: 28 -> 0, of which waited for: 25 -> 0; matrix products, arithmetic and copies ran while one was open for 21% -> 0% of each run, Pallas kernels for 0% -> 0%
where the time goes in v1:
time: 486 us; the launch traced here: 479 us
  Pallas kernels  439 us (90%)
  local copies, waits for them, and re-layouts  22.4 us (5%)
  other arithmetic  11.7 us (2%)
    pallas_call x1, Pallas kernels, back(): pl.pallas_call(functools.partial(back_kernel, slots), in_specs=[ANYWHERE]...  205 us
    pallas_call x1, Pallas kernels, front(): pl.pallas_call(functools.partial(front_kernel, slots), in_specs=[ANYWHERE...  161 us
    pallas_call x1, Pallas kernels, feed_forward(): pl.pallas_call(feed_kernel, grid=(tiles,), in_specs=[whole(heads.shape),...  63.6 us
    unnamed x80, local copies, waits for them, and re-layouts  15.2 us

profile of v1, /device:TPU:0, one launch (start us, length us, event | category | flops | bytes accessed | tf_op | source)
XLA Modules:
  0.0 479.0 jit_solution(4714230270440364762)
XLA Ops:
  0.7 1.1 constant_dynamic-slice_fusion.4
  1.9 1.0 dynamic-slice_bitcast_fusion.1
  2.9 0.8 constant_dynamic-slice_fusion.3
  3.8 1.7 copy.53
  5.7 1.2 copy-done.9
  7.9 1.8 fusion.6.normed_ref
  10.8 161.4 %front.1 = (bf16[2,4,256,1024]{3,2,1,0:T(8,128)(2,1)}, bf16[4,384,1024]{2,1,0:T(8,128)(2,1)}, bf16[6,1024,384]{2,1,0:T(8,128)(2,1)}, bf16[3,4,2,256,128]{4,3,2,1...) custom-call(bf16[3,256,1024]{2,1,0:T(8,128)(2,1)} %fusion.6.normed_r, ...), custom_call_target="tpu_custom_call" | custom-call | flops 40000000000 | bytes 62914560 | tf_op jit(solution)/shard_map/front/pallas_call | solution.py:1048
  172.3 1.1 copy-done.2
  174.0 1.1 copy-done.4
  175.2 0.6 copy-done.5
  175.8 0.6 copy-done.6
  177.6 0.6 pad_maximum_fusion.2.vectors_ref
  178.2 63.6 %feed_forward.1 = (bf16[768,1024]{1,0:T(8,128)(2,1)}, f32[768,1024]{1,0:T(8,128)}, bf16[3,4,2,256,128]{4,3,2,1,0:T(8,128)(2,1)}, bf16[1024,1024]{1,0:T(8,128)(2,...) custom-call(bf16[3,4,2,256,128]{4,3,2,1,0:T(8,128)(2,1)} %copy-done.4, ...), custom_call_target="tpu_custom_call" | custom-call | flops 38654705664 | bytes 60000000 | tf_op jit(solution)/shard_map/feed_forward/pallas_call | solution.py:474
  241.8 0.8 fusion.15
  242.6 0.7 reshape.168
  243.3 0.6 pad_maximum_fusion.1.small_ref
  244.0 0.8 copy.58.rout_ref
  244.7 205.2 %back.1 = (bf16[4,2,384,1024]{3,2,1,0:T(8,128)(2,1)}, bf16[4,256,1024]{2,1,0:T(8,128)(2,1)}, f32[384,128]{1,0:T(8,128)}, f32[80,128]{1,0:T(8,128)}) custom-call(bf16[3,4,2,256,128]{4,3,2,1,0:T(8,128)(2,1)} %get-tuple-element.51.heads_ref, bf16[4,2,4,256,1024]{4,3,2,1,0:T(8,128)(2,1)} %bitcast.93, bf16[4,2,4,32,1024]{4,3,2,1,0:T(8,128)(2,1)} %bitcast.95, ...), custom_call_target="tpu_custom_call" | custom-call | flops 80000000000 | bytes 62914560 | tf_op jit(solution)/shard_map/back/pallas_call | solution.py:1622
  450.0 1.3 slice_bitcast_fusion
  451.3 2.2 convert_element_type.26
  454.0 0.9 copy-done.10
  454.9 1.1 fusion.14
  456.1 2.3 fusion.10
  458.4 6.2 %write_feed.1 = (f32[1024,1024]{1,0:T(8,128)}, f32[1024,1024]{1,0:T(8,128)}) custom-call(bf16[4,2,384,1024]{3,2,1,0:T(8,128)(2,1)} %get-tuple-element.65.piece_ref), custom_call_target="tpu_custom_call" | custom-call | tf_op jit(solution)/shard_map/write_feed/pallas_call | solution.py:1695
  464.6 1.0 convolution_bitcast_fusion
  465.7 1.8 copy.61
  467.5 2.8 copy-done.1
  470.3 3.0 write_rest.1
  474.1 0.9 fusion.16
  475.0 1.6 fusion.22
  476.7 0.7 reshape.170
  478.0 0.6 constant_dynamic-slice_fusion.1
  (103 shorter events, 6.0 us)
Async XLA Ops:
  0.7 9.0 %copy-start = (bf16[1024,512]{1,0:T(8,128)(2,1)S(1)}, bf16[1024,512]{1,0:T(8,128)(2,1)}, u32[]{:S(2)}) copy-start(bf16[1024,512]{1,0:T(8,128)(2,1)} %param.37) | copy-start | bytes 3145732
  5.5 1.4 copy-start.9
  5.5 2.4 copy-start.24
  5.5 2.4 copy-start.27
  6.9 2.8 copy-start.17
  6.9 2.8 copy-start.34
  7.2 2.8 copy-start.15
  7.2 2.8 copy-start.35
  7.2 2.9 copy-start.36
  7.2 3.0 copy-start.26
  7.2 3.4 copy-start.28
  7.2 3.5 copy-start.29
  7.3 2.9 copy-start.19
  7.9 2.3 copy-start.21
  10.8 166.8 %copy-start.30 = (f32[1024]{0:T(1024)S(1)}, f32[1024]{0:T(1024)}, u32[]{:S(2)}) copy-start(f32[1024]{0:T(1024)} %param.35) | copy-start | bytes 12292
  10.8 166.8 %copy-start.31 = (f32[1024]{0:T(1024)S(1)}, f32[1024]{0:T(1024)}, u32[]{:S(2)}) copy-start(f32[1024]{0:T(1024)} %param.31) | copy-start | bytes 12292
  10.8 166.8 %copy-start.32 = (f32[1024]{0:T(1024)S(1)}, f32[1024]{0:T(1024)}, u32[]{:S(2)}) copy-start(f32[1024]{0:T(1024)} %param.30) | copy-start | bytes 12292
  10.8 166.8 %copy-start.33 = (f32[1024]{0:T(1024)S(1)}, f32[1024]{0:T(1024)}, u32[]{:S(2)}) copy-start(f32[1024]{0:T(1024)} %param.29) | copy-start | bytes 12292
  172.3 1.1 copy-start.2
  174.0 1.1 copy-start.4
  175.2 0.6 copy-start.5
  451.3 2.4 copy-start.11
  453.5 1.4 copy-start.10
  453.5 1.4 copy-start.20
  453.5 1.4 copy-start.22
  453.5 1.4 copy-start.25
  454.0 2.1 copy-start.12
  458.4 6.2 %copy-start.23 = (f32[80,128]{1,0:T(8,128)S(1)}, f32[80,128]{1,0:T(8,128)}, u32[]{:S(2)}) copy-start(f32[80,128]{1,0:T(8,128)} %get-tuple-element.64) | copy-start | bytes 122884
  458.4 6.2 %copy-start.14 = (f32[10,512]{1,0:T(8,128)S(1)}, f32[10,512]{1,0:T(8,128)}, u32[]{:S(2)}) copy-start(f32[10,512]{1,0:T(8,128)} %copy-done.13) | copy-start | bytes 61444
  458.4 6.3 %copy-start.18 = (bf16[10,1024]{1,0:T(8,128)(2,1)S(1)}, bf16[10,1024]{1,0:T(8,128)(2,1)}, u32[]{:S(2)}) copy-start(bf16[10,1024]{1,0:T(8,128)(2,1)} %param.36) | copy-start | bytes 61444
  467.5 2.8 copy-start.1
  470.3 3.0 copy-start.16
  (5 other events, 3.0 us)

commit v2 on v1

--- a/solution.py
+++ b/solution.py
@@ -364,7 +364,7 @@
 
 
 def feed_kernel(
-    heads_ref, tokens_ref, cot_ref, out_own_ref, out_ref, vectors_ref,
+    heads_ref, tokens_ref, cot_ref, out_own_ref, out_ref, obias_ref, gain_ref, offset_ref, dbias_ref,
     own_up_ref, own_down_ref, weight_ref, bias_ref,
     block_ref, resid_ref, dheads_ref, gout_ref, sums_ref, grad_ref, gbias_ref,
     heads_s, normed_s, resid_s, mlp_s, dn_s,
@@ -372,7 +372,7 @@
     step = pl.program_id(0)
     blocks, near, cores, share, lanes = heads_ref.shape
     own_rows = out_own_ref.shape[0]
-    out_bias, gain, offset, down_bias = [vectors_ref[j : j + 1] for j in range(4)]
+    out_bias, gain, offset, down_bias = obias_ref[...], gain_ref[...], offset_ref[...], dbias_ref[...]
 
     @pl.when(step == 0)
     def _before():
@@ -480,7 +480,7 @@
             whole(square),
             whole(out_own.shape),
             whole(out.shape),
-            whole(vectors.shape),
+            *[whole((1, width))] * 4,
             pl.BlockSpec((width, depth // 2), lambda i: (0, i)),
             pl.BlockSpec((1, depth // 2, width), lambda i: (i, 0, 0)),
             pl.BlockSpec((1, others, depth, width), lambda i: (i, 0, 0, 0)),
@@ -517,7 +517,7 @@
             transcendentals=rows * tiles * units,
         ),
         name="feed_forward",
-    )(heads, tokens, cot, out_own, out, vectors, own_up, own_down, weights, bias)
+    )(heads, tokens, cot, out_own, out, *vectors, own_up, own_down, weights, bias)
 
 
 MESH_IDS = pl.DeviceIdType.MESH
@@ -1170,12 +1170,12 @@
 def back_kernel(
     slots,
     heads_ref, feed_ref, proj_ref, qkv_ref, rows_ref, weight_ref,
-    log_ref, tab_ref, seg_ref, live_ref, small_ref, tokens_ref, rout_ref,
+    log_ref, tab_ref, seg_ref, live_ref, upb_ref, norms_ref, tokens_ref, rout_ref,
     full_out, back_out, first_out, second_out,
     sends, recvs, local,
     dh_v, sib_v, own_v, plane_v, sum_v, z_v, gq_v, plane_q, sum_q, z_q, done_v,
     qkv_v, weight_v, df_v, dfs_v, col_v, dk_acc, dv_acc,
-    dtab_v, dbias_v, back_v, first_v, first_in, second_v, second_in,
+    dtab_v, dbias_v, back_v, first_v, first_in, second_v, second_in, dfm_v,
 ):
     plane, core, zed = position()
     parity = lax.rem(zed, 2)
@@ -1324,17 +1324,25 @@
     ]
 
     def small_send(name, values, arrived, step):
-        wires.put(values.at[step], arrived.at[step], slot(name, step), partners[step])
+        source = arrived.at[step - 1] if step else values.at[0]
+        wires.put(source, arrived.at[step], slot(name, step), partners[step])
 
     def small_take(name, values, arrived, step):
         wires.got(arrived.at[step], slot(name, step), partners[step])
-        values[step + 1] = values[step] + arrived[step]
+        arrived[step] = arrived[step] + (arrived[step - 1] if step else values[0])
         if step < 4:
             small_send(name, values, arrived, step + 1)
 
     def first_sums():
         first_v[0] = jnp.zeros(first_v.shape[1:], jnp.float32)
-        first_v[0, :64] = small_ref[...]
+        for at in range(8):
+            for step in range(4):
+                line = upb_ref[at, :, 128 * step : 128 * step + 128]
+                first_v[0, pl.ds(4 * at + ahead[step], 1)] = line
+        for at in range(4):
+            for j in range(8):
+                line = norms_ref[at : at + 1, 128 * j : 128 * j + 128]
+                first_v[0, 32 + 8 * at + j : 33 + 8 * at + j] = line
         for at in range(4):
             entry = core * 4 + lax.rem(at + 2 * parity, 4)
             table, bias = dtab_v[at], dbias_v[at]
@@ -1352,7 +1360,7 @@
     def tanh_part():
         entry = lax.div(plane, 2) * 4 + zed
         base = pl.multiple_of(64 + 32 * entry + 16 * core, 8)
-        table = first_v[5, pl.ds(base, 16)]
+        table = first_in[4, pl.ds(base, 16)]
         table = jnp.where(lax.rem(plane, 2) == 0, table[:, :HEAD_DIM], table[:, HEAD_DIM:])
         part = lax.dot_general(
             table,
@@ -1390,6 +1398,15 @@
     first_row = slot("r", 0)
     for number in range(1, 4):
         slot("r", number)
+
+    far_home = jnp.logical_or(zed == 0, zed == 3)
+    other_home = zed + 1 - 2 * parity
+    outside = lax.div(zed, 2) != core
+    far_place = 1 + 2 * core
+
+    @pl.when(outside)
+    def _nothing():
+        back_v[far_place] = jnp.zeros(back_v.shape[1:], jnp.bfloat16)
 
     def row_grads(kind):
         for quarter in range(4):
@@ -1415,9 +1432,27 @@
             def _sum():
                 add_up(share, dfs_v.at[quarter], dfs_v.at[quarter], df_v.at[kind, quarter])
 
+        if kind:
+            for j in range(2):
+                z_out = 2 - 2 * origin + j
+                wires.put_if(
+                    jnp.logical_and(here, far_home), dfs_v.at[z_out], dfm_v.at[j], slot("m", j),
+                    (plane, core, other_home),
+                )
+                joins = jnp.logical_and(here, jnp.logical_not(far_home))
+                wires.got_if(joins, dfm_v.at[j], slot("m", j), (plane, core, other_home))
+
+                @pl.when(joins)
+                def _join():
+                    add_up(share, dfs_v.at[z_out], dfs_v.at[z_out], dfm_v.at[j])
+
         for step in range(4):
             z_to = lax.rem(2 * parity + kind + 4 - step, 4)
             own = jnp.logical_and(origin == core, z_to == zed)
+            goes = here
+            if kind:
+                beyond = jnp.logical_and(far_home, lax.div(z_to, 2) != origin)
+                goes = jnp.logical_and(here, jnp.logical_not(beyond))
             source, target = dfs_v.at[z_to], back_v.at[2 * parity + kind]
 
             @pl.when(jnp.logical_and(here, own))
@@ -1425,7 +1460,7 @@
                 pltpu.make_async_copy(source, target, recvs.at[first_row + step]).start()
 
             wires.put_if(
-                jnp.logical_and(here, jnp.logical_not(own)),
+                jnp.logical_and(goes, jnp.logical_not(own)),
                 source,
                 target,
                 first_row + step,
@@ -1572,7 +1607,8 @@
         )
     spread_on("f", feed_span)
     for k in range(4):
-        wires.got(
+        wires.got_if(
+            jnp.logical_not(jnp.logical_and(outside, far_place == k)),
             back_v.at[k],
             first_row + lax.rem(k + 4 - zed, 4),
             (plane, k % 2, 2 * core + k // 2),
@@ -1597,8 +1633,8 @@
     spread_far("q", q_span)
     small_take("b", second_v, second_in, 3)
     small_take("b", second_v, second_in, 4)
-    first_out[...] = first_v[5]
-    second_out[...] = second_v[5]
+    first_out[...] = first_in[4]
+    second_out[...] = second_in[4]
     spread_end("f", feed_span)
     spread_end("q", q_span)
     for copy in last:
@@ -1607,11 +1643,11 @@
     assert len(slot_at) == BACK_COPIES, len(slot_at)
 
 
-BACK_COPIES = 98
+BACK_COPIES = 100
 
 
 def back(
-    slots, d_heads, grad_feed, grad_out, qkv, rows, weights, logs, tab, seg, live, small, tokens, rout
+    slots, d_heads, grad_feed, grad_out, qkv, rows, weights, logs, tab, seg, live, upb, norms, tokens, rout
 ):
     bf16, f32 = jnp.bfloat16, jnp.float32
     share, width = rows.shape[2:]
@@ -1621,7 +1657,7 @@
     both, q_rows = grad_feed.shape[3] + grad_out.shape[3], 96
     return pl.pallas_call(
         functools.partial(back_kernel, slots),
-        in_specs=[ANYWHERE] * 6 + [vmem] * 7,
+        in_specs=[ANYWHERE] * 6 + [vmem] * 8,
         out_specs=[ANYWHERE] * 2 + [vmem] * 2,
         out_shape=[
             shaped((4, 2, both + q_rows, width), bf16),
@@ -1654,10 +1690,11 @@
             held((PAIRS, 16, 256), f32),
             held((PAIRS, 1, 384), f32),
             held((4, share, width), bf16),
-            held((6, 384, 128), f32),
+            held((1, 384, 128), f32),
             held((5, 384, 128), f32),
-            held((6, 80, 128), f32),
+            held((1, 80, 128), f32),
             held((5, 80, 128), f32),
+            held((2, share, width), bf16),
         ],
         compiler_params=pltpu.CompilerParams(
             collective_id=2, has_side_effects=True, vmem_limit_bytes=62 << 20
@@ -1667,7 +1704,7 @@
         ),
         name="back",
     )(
-        d_heads, grad_feed, grad_out, qkv, rows, weights, logs, tab, seg, live, small, tokens, rout
+        d_heads, grad_feed, grad_out, qkv, rows, weights, logs, tab, seg, live, upb, norms, tokens, rout
     )
 
 
@@ -1687,6 +1724,33 @@
     grad_ref[...] = jnp.concatenate(
         [turned[:, 128 * kind + 64 * head : 128 * kind + 64 * head + 64] for kind, head in order], 1
     )
+
+
+def last_kernel(came_ref, tokens_ref, resid_ref, gain_ref, grad_ref):
+    row = pl.program_id(0)
+    grad = came_ref[row].astype(jnp.float32) + jnp.where(
+        row == 1, came_ref[3].astype(jnp.float32), 0.0
+    )
+    hat, inverse = normalize(tokens_ref[0].astype(jnp.float32))
+    grad_ref[0] = resid_ref[0] + norm_back(grad, hat, inverse, gain_ref[...])
+
+
+def last_norm(came, tokens, d_resid, gain):
+    rows = pl.BlockSpec((1, *tokens.shape[1:]), lambda m: (m, 0, 0))
+    return pl.pallas_call(
+        last_kernel,
+        grid=(tokens.shape[0],),
+        in_specs=[
+            pl.BlockSpec(came.shape, lambda m: (0, 0, 0)),
+            rows,
+            rows,
+            pl.BlockSpec((1, tokens.shape[2]), lambda m: (0, 0)),
+        ],
+        out_specs=rows,
+        out_shape=jax.ShapeDtypeStruct(tokens.shape, jnp.float32),
+        compiler_params=pltpu.CompilerParams(vmem_limit_bytes=32 << 20),
+        name="last_norm",
+    )(came, tokens, d_resid, gain)
 
 
 def write_grads(full):
@@ -1806,7 +1870,7 @@
         cotangent.reshape(3 * share, width),
         out_weight,
         out_full.reshape(3 * 256, width),
-        jnp.stack([out_bias, ln2_gain, ln2_bias, down_bias]),
+        [vector.reshape(1, width) for vector in (out_bias, ln2_gain, ln2_bias, down_bias)],
         up_weight,
         down_own,
         feed_full.reshape(8, 3, 256, width),
@@ -1815,12 +1879,6 @@
     block_out = block_out.reshape(tokens.shape)
     grad_feed = grad_feed.reshape(4, 2, 4, 256, width)
     grad_out = grad_out.reshape(4, 2, 4, 32, width)
-    small = jnp.concatenate(
-        [
-            jnp.roll(grad_up_bias.reshape(8, 4, 128), zed, 1).reshape(32, 128),
-            sums.reshape(32, 128),
-        ]
-    )
     full, came, first, second = back(
         slots,
         d_heads,
@@ -1833,14 +1891,13 @@
         tab,
         seg,
         live,
-        small,
+        grad_up_bias,
+        sums,
         tokens,
         reparam_out,
     )
-    came = came.astype(f32)
-    d_first = jnp.stack([came[0], came[1] + came[3], came[2]])
-    input_grad = d_resid.reshape(tokens.shape) + norm_back(
-        d_first, hat_first, inverse_first, ln1_gain
+    input_grad = last_norm(
+        came, tokens, d_resid.reshape(tokens.shape), ln1_gain.reshape(1, width)
     )
     grad_up, grad_down, grad_out, grad_qkv = write_grads(full)
     grad_up_bias = pick(first[:32].reshape(8, 4, 128).transpose(1, 0, 2).reshape(4, 1024), zed)

time: 486 us -> 463 us (0.953)
  Pallas kernels: 439 us -> 424 us
  other arithmetic: 11.7 us -> 3.83 us
    pallas_call x1, Pallas kernels: 205 us -> 186 us  [back(): pl.pallas_call(functools.partial(back_kernel, slots), in_specs=[ANYWHERE]...]
    unnamed x80 -> x64, local copies, waits for them, and re-layouts: 15.2 us -> 15.6 us
where the time goes in v2:
time: 463 us; the launch traced here: 454 us
  Pallas kernels  424 us (92%)
  local copies, waits for them, and re-layouts  21.1 us (5%)
    pallas_call x1, Pallas kernels, back(): pl.pallas_call(functools.partial(back_kernel, slots), in_specs=[ANYWHERE]...  186 us
    pallas_call x1, Pallas kernels, front(): pl.pallas_call(functools.partial(front_kernel, slots), in_specs=[ANYWHERE...  161 us
    pallas_call x1, Pallas kernels, feed_forward(): pl.pallas_call(feed_kernel, grid=(tiles,), in_specs=[whole(heads.shape),...  63.6 us
    unnamed x64, local copies, waits for them, and re-layouts  15.6 us

profile of v2, /device:TPU:0, one launch (start us, length us, event | category | flops | bytes accessed | tf_op | source)
XLA Modules:
  0.0 454.1 jit_solution(17785634439358931921)
XLA Ops:
  0.7 1.1 constant_dynamic-slice_fusion.4
  1.9 1.0 dynamic-slice_bitcast_fusion.1
  2.9 0.8 constant_dynamic-slice_fusion.3
  3.8 1.7 copy.53
  5.7 0.6 copy-done.19
  6.5 0.6 copy-done.15
  7.6 0.6 fusion.2
  8.2 1.8 fusion.5.normed_ref
  10.3 161.3 %front.1 = (bf16[2,4,256,1024]{3,2,1,0:T(8,128)(2,1)}, bf16[4,384,1024]{2,1,0:T(8,128)(2,1)}, bf16[6,1024,384]{2,1,0:T(8,128)(2,1)}, bf16[3,4,2,256,128]{4,3,2,1...) custom-call(bf16[3,256,1024]{2,1,0:T(8,128)(2,1)} %fusion.5.normed_r, ...), custom_call_target="tpu_custom_call" | custom-call | flops 40000000000 | bytes 62914560 | tf_op jit(solution)/shard_map/front/pallas_call | solution.py:1048
  171.7 1.1 copy-done.8
  172.8 0.6 copy-done.9
  173.4 1.1 copy-done.10
  174.6 0.6 copy-done.11
  175.2 0.6 copy-done.12
  175.8 0.6 copy-done.13
  176.4 0.6 copy-done.14
  177.0 63.6 %feed_forward.1 = (bf16[768,1024]{1,0:T(8,128)(2,1)}, f32[768,1024]{1,0:T(8,128)}, bf16[3,4,2,256,128]{4,3,2,1,0:T(8,128)(2,1)}, bf16[1024,1024]{1,0:T(8,128)(2,...) custom-call(bf16[3,4,2,256,128]{4,3,2,1,0:T(8,128)(2,1)} %copy-done.10, ...), custom_call_target="tpu_custom_call" | custom-call | flops 38654705664 | bytes 60000000 | tf_op jit(solution)/shard_map/feed_forward/pallas_call | solution.py:474
  240.7 0.8 copy.58.rout_ref
  241.4 186.0 %back.1 = (bf16[4,2,384,1024]{3,2,1,0:T(8,128)(2,1)}, bf16[4,256,1024]{2,1,0:T(8,128)(2,1)}, f32[384,128]{1,0:T(8,128)}, f32[80,128]{1,0:T(8,128)}) custom-call(bf16[3,4,2,256,128]{4,3,2,1,0:T(8,128)(2,1)} %get-tuple-element.50.heads_ref, bf16[4,2,4,256,1024]{4,3,2,1,0:T(8,128)(2,1)} %bitcast.91, bf16[4,2,4,32,1024]{4,3,2,1,0:T(8,128)(2,1)} %bitcast.93, ...), custom_call_target="tpu_custom_call" | custom-call | flops 80000000000 | bytes 62914560 | tf_op jit(solution)/shard_map/back/pallas_call | solution.py:1658
  427.5 6.2 %write_feed.1 = (f32[1024,1024]{1,0:T(8,128)}, f32[1024,1024]{1,0:T(8,128)}) custom-call(bf16[4,2,384,1024]{3,2,1,0:T(8,128)(2,1)} %get-tuple-element.65.piece_ref), custom_call_target="tpu_custom_call" | custom-call | tf_op jit(solution)/shard_map/write_feed/pallas_call | solution.py:1759
  433.7 1.0 convolution_bitcast_fusion
  434.8 1.8 copy.61
  436.6 2.8 copy-done.1
  439.4 3.0 write_rest.1
  442.4 0.6 slice_bitcast_fusion
  443.3 1.6 copy-done.5
  444.8 3.5 last_norm.1
  449.2 0.9 fusion.8
  450.1 1.6 fusion.14
  451.8 0.7 reshape.170
  452.5 0.6 fusion.13
  453.1 0.6 constant_dynamic-slice_fusion.1
  (78 shorter events, 2.5 us)
Async XLA Ops:
  0.7 5.0 %copy-start = (bf16[1024,512]{1,0:T(8,128)(2,1)S(1)}, bf16[1024,512]{1,0:T(8,128)(2,1)}, u32[]{:S(2)}) copy-start(bf16[1024,512]{1,0:T(8,128)(2,1)} %param.37) | copy-start | bytes 3145732
  5.5 0.8 copy-start.19
  5.5 0.8 copy-start.26
  5.5 1.6 copy-start.17
  5.5 1.6 copy-start.27
  5.5 1.7 copy-start.2
  6.3 2.0 copy-start.6
  6.3 2.0 copy-start.23
  6.5 0.6 copy-start.15
  7.6 2.4 copy-start.28
  7.6 2.5 copy-start.22
  7.6 2.5 copy-start.24
  7.6 2.7 copy-start.25
  171.7 1.1 copy-start.8
  172.8 0.6 copy-start.9
  173.4 1.1 copy-start.10
  174.6 0.6 copy-start.11
  175.2 0.6 copy-start.12
  175.8 0.6 copy-start.13
  176.4 0.6 copy-start.14
  427.5 6.2 %copy-start.21 = (f32[80,128]{1,0:T(8,128)S(1)}, f32[80,128]{1,0:T(8,128)}, u32[]{:S(2)}) copy-start(f32[80,128]{1,0:T(8,128)} %get-tuple-element.64) | copy-start | bytes 122884
  427.5 6.2 %copy-start.16 = (f32[10,512]{1,0:T(8,128)S(1)}, f32[10,512]{1,0:T(8,128)}, u32[]{:S(2)}) copy-start(f32[10,512]{1,0:T(8,128)} %copy-done.15) | copy-start | bytes 61444
  427.5 6.2 %copy-start.20 = (bf16[10,1024]{1,0:T(8,128)(2,1)S(1)}, bf16[10,1024]{1,0:T(8,128)(2,1)}, u32[]{:S(2)}) copy-start(bf16[10,1024]{1,0:T(8,128)(2,1)} %param.36) | copy-start | bytes 61444
  436.6 2.8 copy-start.1
  439.4 3.0 copy-start.18
  439.4 3.7 copy-start.3
  439.4 3.9 copy-start.4
  439.4 3.9 copy-start.7
  443.3 1.6 copy-start.5

commit v3 on v2

--- a/solution.py
+++ b/solution.py
@@ -1333,6 +1333,21 @@
         if step < 4:
             small_send(name, values, arrived, step + 1)
 
+    half_rows = first_v.shape[1] // 2
+    mine_rows = pl.ds(pl.multiple_of(core * half_rows, 8), half_rows)
+    other_rows = pl.ds(pl.multiple_of((1 - core) * half_rows, 8), half_rows)
+
+    def first_take(step):
+        if step == 5:
+            wires.got(first_in.at[4, other_rows], slot("a", 5), sibling)
+            return
+        here = first_in.at[step, mine_rows]
+        wires.got(here, slot("a", step), partners[step])
+        before = first_in[step - 1, mine_rows] if step else first_v[0, mine_rows]
+        first_in[step, mine_rows] = first_in[step, mine_rows] + before
+        at, there = (step + 1, partners[step + 1]) if step < 4 else (4, sibling)
+        wires.put(here, first_in.at[at, mine_rows], slot("a", step + 1), there)
+
     def first_sums():
         first_v[0] = jnp.zeros(first_v.shape[1:], jnp.float32)
         for at in range(8):
@@ -1355,7 +1370,7 @@
             first_v[0, pl.ds(base, 8)] = jnp.concatenate(
                 [bias[:, :128], bias[:, 128:256], bias[:, 256:], jnp.zeros((5, 128), jnp.float32)], 0
             )
-        small_send("a", first_v, first_in, 0)
+        wires.put(first_v.at[0, other_rows], first_in.at[0, other_rows], slot("a", 0), sibling)
 
     def tanh_part():
         entry = lax.div(plane, 2) * 4 + zed
@@ -1489,7 +1504,7 @@
     send_rows(0)
     row_grads(1)
     plane_sum(2)
-    small_take("a", first_v, first_in, 0)
+    first_take(0)
     row_copy.wait()
     rows_a = jnp.concatenate([rows_v[0, j, :share] for j in range(4)], 0)
     for at in range(4):
@@ -1512,10 +1527,10 @@
                     slot("pq", sub, kind),
                     around[first],
                 )
-    small_take("a", first_v, first_in, 1)
+    first_take(1)
     send_rows(1)
     plane_sum(3)
-    small_take("a", first_v, first_in, 2)
+    first_take(2)
     for sub in range(2):
         first, other = axes(sub)
         slots_here = slice(2 * sub, 2 * sub + 2)
@@ -1527,7 +1542,7 @@
         wires.put(
             gq_v.at[slots_here, at_other], plane_q.at[2, slots_here], slot("pq", sub, 2), around[other]
         )
-    small_take("a", first_v, first_in, 3)
+    first_take(3)
 
     def spread(name, span_of):
         copy = pltpu.make_async_copy(
@@ -1590,8 +1605,7 @@
         wires.got(z_v.at[turn], slot("z", turn), (plane, core, lax.rem(zed + 3 - turn, 4)))
     add_up(both, done_v.at[feed_span(2)], sum_v.at[3], *[z_v.at[j] for j in range(3)])
     last = [spread("f", feed_span)]
-    small_take("a", first_v, first_in, 4)
-    tanh_part()
+    first_take(4)
     for sub in range(2):
         slots_here = slice(2 * sub, 2 * sub + 2)
         for kind, offset in zip((1, 2), axes(sub)):
@@ -1605,6 +1619,8 @@
             slot("zq", turn),
             (plane, core, turns[turn]),
         )
+    first_take(5)
+    tanh_part()
     spread_on("f", feed_span)
     for k in range(4):
         wires.got_if(
@@ -1643,7 +1659,7 @@
     assert len(slot_at) == BACK_COPIES, len(slot_at)
 
 
-BACK_COPIES = 100
+BACK_COPIES = 101
 
 
 def back(

time: 463 us -> 462 us (level)
  no operation moved by 1% of the time
where the time goes in v3:
time: 462 us; the launch traced here: 456 us
  Pallas kernels  425 us (92%)
  local copies, waits for them, and re-layouts  21.1 us (5%)
    pallas_call x1, Pallas kernels, back(): pl.pallas_call(functools.partial(back_kernel, slots), in_specs=[ANYWHERE]...  188 us
    pallas_call x1, Pallas kernels, front(): pl.pallas_call(functools.partial(front_kernel, slots), in_specs=[ANYWHERE...  161 us
    pallas_call x1, Pallas kernels, feed_forward(): pl.pallas_call(feed_kernel, grid=(tiles,), in_specs=[whole(heads.shape),...  63.6 us
    unnamed x64, local copies, waits for them, and re-layouts  15.6 us

profile of v3, /device:TPU:0, one launch (start us, length us, event | category | flops | bytes accessed | tf_op | source)
XLA Modules:
  0.0 455.6 jit_solution(11387038470044258617)
XLA Ops:
  0.7 1.1 constant_dynamic-slice_fusion.4
  1.9 1.0 dynamic-slice_bitcast_fusion.1
  2.9 0.8 constant_dynamic-slice_fusion.3
  3.8 1.7 copy.53
  5.7 0.6 copy-done.19
  6.5 0.6 copy-done.15
  7.6 0.6 fusion.2
  8.2 1.8 fusion.5.normed_ref
  10.3 161.3 %front.1 = (bf16[2,4,256,1024]{3,2,1,0:T(8,128)(2,1)}, bf16[4,384,1024]{2,1,0:T(8,128)(2,1)}, bf16[6,1024,384]{2,1,0:T(8,128)(2,1)}, bf16[3,4,2,256,128]{4,3,2,1...) custom-call(bf16[3,256,1024]{2,1,0:T(8,128)(2,1)} %fusion.5.normed_r, ...), custom_call_target="tpu_custom_call" | custom-call | flops 40000000000 | bytes 62914560 | tf_op jit(solution)/shard_map/front/pallas_call | solution.py:1048
  171.7 1.1 copy-done.8
  172.8 0.6 copy-done.9
  173.4 1.1 copy-done.10
  174.6 0.6 copy-done.11
  175.2 0.6 copy-done.12
  175.8 0.6 copy-done.13
  176.4 0.6 copy-done.14
  177.0 63.6 %feed_forward.1 = (bf16[768,1024]{1,0:T(8,128)(2,1)}, f32[768,1024]{1,0:T(8,128)}, bf16[3,4,2,256,128]{4,3,2,1,0:T(8,128)(2,1)}, bf16[1024,1024]{1,0:T(8,128)(2,...) custom-call(bf16[3,4,2,256,128]{4,3,2,1,0:T(8,128)(2,1)} %copy-done.10, ...), custom_call_target="tpu_custom_call" | custom-call | flops 38654705664 | bytes 60000000 | tf_op jit(solution)/shard_map/feed_forward/pallas_call | solution.py:474
  240.7 0.8 copy.58.rout_ref
  241.4 187.6 %back.1 = (bf16[4,2,384,1024]{3,2,1,0:T(8,128)(2,1)}, bf16[4,256,1024]{2,1,0:T(8,128)(2,1)}, f32[384,128]{1,0:T(8,128)}, f32[80,128]{1,0:T(8,128)}) custom-call(bf16[3,4,2,256,128]{4,3,2,1,0:T(8,128)(2,1)} %get-tuple-element.50.heads_ref, bf16[4,2,4,256,1024]{4,3,2,1,0:T(8,128)(2,1)} %bitcast.91, bf16[4,2,4,32,1024]{4,3,2,1,0:T(8,128)(2,1)} %bitcast.93, ...), custom_call_target="tpu_custom_call" | custom-call | flops 80000000000 | bytes 62914560 | tf_op jit(solution)/shard_map/back/pallas_call | solution.py:1674
  429.0 6.2 %write_feed.1 = (f32[1024,1024]{1,0:T(8,128)}, f32[1024,1024]{1,0:T(8,128)}) custom-call(bf16[4,2,384,1024]{3,2,1,0:T(8,128)(2,1)} %get-tuple-element.65.piece_ref), custom_call_target="tpu_custom_call" | custom-call | tf_op jit(solution)/shard_map/write_feed/pallas_call | solution.py:1775
  435.3 1.0 convolution_bitcast_fusion
  436.3 1.8 copy.61
  438.1 2.8 copy-done.1
  440.9 3.0 write_rest.1
  444.0 0.6 slice_bitcast_fusion
  444.8 1.6 copy-done.5
  446.4 3.5 last_norm.1
  450.7 0.9 fusion.8
  451.6 1.6 fusion.14
  453.3 0.7 reshape.170
  454.0 0.6 fusion.13
  454.6 0.6 constant_dynamic-slice_fusion.1
  (78 shorter events, 2.5 us)
Async XLA Ops:
  0.7 5.0 %copy-start = (bf16[1024,512]{1,0:T(8,128)(2,1)S(1)}, bf16[1024,512]{1,0:T(8,128)(2,1)}, u32[]{:S(2)}) copy-start(bf16[1024,512]{1,0:T(8,128)(2,1)} %param.37) | copy-start | bytes 3145732
  5.5 0.8 copy-start.19
  5.5 0.8 copy-start.26
  5.5 1.6 copy-start.17
  5.5 1.6 copy-start.27
  5.5 1.7 copy-start.2
  6.3 2.0 copy-start.6
  6.3 2.0 copy-start.23
  6.5 0.6 copy-start.15
  7.6 2.4 copy-start.28
  7.6 2.5 copy-start.22
  7.6 2.5 copy-start.24
  7.6 2.7 copy-start.25
  171.7 1.1 copy-start.8
  172.8 0.6 copy-start.9
  173.4 1.1 copy-start.10
  174.6 0.6 copy-start.11
  175.2 0.6 copy-start.12
  175.8 0.6 copy-start.13
  176.4 0.6 copy-start.14
  429.0 6.2 %copy-start.21 = (f32[80,128]{1,0:T(8,128)S(1)}, f32[80,128]{1,0:T(8,128)}, u32[]{:S(2)}) copy-start(f32[80,128]{1,0:T(8,128)} %get-tuple-element.64) | copy-start | bytes 122884
  429.0 6.2 %copy-start.16 = (f32[10,512]{1,0:T(8,128)S(1)}, f32[10,512]{1,0:T(8,128)}, u32[]{:S(2)}) copy-start(f32[10,512]{1,0:T(8,128)} %copy-done.15) | copy-start | bytes 61444
  429.0 6.2 %copy-start.20 = (bf16[10,1024]{1,0:T(8,128)(2,1)S(1)}, bf16[10,1024]{1,0:T(8,128)(2,1)}, u32[]{:S(2)}) copy-start(bf16[10,1024]{1,0:T(8,128)(2,1)} %param.36) | copy-start | bytes 61444
  438.1 2.8 copy-start.1
  440.9 3.0 copy-start.18
  440.9 3.7 copy-start.3
  440.9 3.9 copy-start.4
  440.9 3.9 copy-start.7
  444.8 1.6 copy-start.5
